TPU v7x, 512 devices: a whole 4x8x8 slice. The times are simulated.
512 devices in a mesh: pipe: 64 (over y, z_lo, core), expert: 8 (over x, z_hi).
Axes of the slice: x: 4, y: 8, z: 8 (z_hi: 2, z_lo: 4; z = z_hi * 4 + z_lo), core: 2. Of those that a mesh axis runs over, the one named last changes fastest.
Arguments:
- forward_input: bfloat16 [64, 128, 4096], P('pipe', 'expert'), may hold values from -6 to 6
- forward_route: int32 [64, 128, 2], P('pipe', 'expert'), may hold values from 0 to 7, as said below
- forward_gates: float32 [64, 128, 2], P('pipe', 'expert'), may hold values from 0.2 to 2
- backward_cotangent: bfloat16 [64, 128, 4096], P('pipe', 'expert'), may hold values from -6 to 6
- backward_route: int32 [64, 128, 2], P('pipe', 'expert'), may hold values from 0 to 7, as said below
- backward_gates: float32 [64, 128, 2], P('pipe', 'expert'), may hold values from 0.2 to 2
- gate_up_weight: bfloat16 [64, 8, 2048, 512], P('pipe', 'expert'), may hold values from -0.09375 to 0.09375
- down_weight: bfloat16 [64, 8, 1024, 512], P('pipe', 'expert'), may hold values from -0.1875 to 0.1875
- saved_projections: bfloat16 [64, 8, 576, 256], P('pipe', 'expert'), may hold values from -4 to 4
Outputs:
- next_input: bfloat16 [64, 128, 4096], P('pipe', 'expert')
- prior_gradient: bfloat16 [64, 128, 4096], P('pipe', 'expert')
Inputs may be any that keep to these rules, and one draw needn't show every extreme that they name: `forward_route`: each token names 2 different experts. In every section one expert, drawn afresh for each section, is named by exactly 9 tokens of every source; each other expert by at most 4 tokens of one source, the remaining choices of a source being spread over the other experts as evenly as possible. `backward_route`: as for forward_route, with its own busiest experts.
All inputs are finite; a program needn't handle non-finite values.
Results may differ from a plain program's by a relative error of at most 0.0058.
Values may be sent and summed in bfloat16 or wider, within the bound.
A program may use at most 64 MiB of HBM per device.

v0:
```python
import jax
import jax.numpy as jnp
from jax import lax
from jax.sharding import PartitionSpec as P

GROUP = 8


def partner(value, axis, stride):
    mask = 2**stride
    pairs = [(source, source ^ mask) for source in range(lax.axis_size(axis))]
    return lax.ppermute(value, axis, pairs)


def passed_along(array, axis, by):
    count = lax.axis_size(axis)
    return lax.ppermute(array, axis, [(i, (i + by) % count) for i in range(count)])


def silu_terms(gate_pre):
    logistic = jax.nn.sigmoid(gate_pre)
    return (gate_pre * logistic, logistic * (1.0 + gate_pre * (1.0 - logistic)))


def rank_slots(route, experts):
    labels = lax.broadcasted_iota(jnp.int32, (1, 1, experts), 2)
    hits = (route[:, :, None] == labels).astype(jnp.int32)
    row_hits = jnp.sum(hits, axis=1)
    before = jnp.cumsum(row_hits, axis=0) - row_hits
    return jnp.sum(hits * before[:, None, :], axis=2)


def slot_table(route, slot_rank, capacity, experts):
    tokens_here = route.shape[0]
    target = route * capacity + slot_rank
    row_ids = lax.broadcasted_iota(jnp.int32, route.shape, 0)
    source_rows = jnp.full((experts * capacity,), tokens_here, jnp.int32)
    return source_rows.at[target.reshape(-1)].set(row_ids.reshape(-1), mode="drop")


def gather_rows(values, source_rows):
    return jnp.take(values, source_rows, axis=0, mode="fill", fill_value=0)


def combine_rows(flat_out, position, gates):
    gathered = jnp.take(flat_out, position, axis=0).astype(jnp.float32)
    return jnp.sum(gathered * gates[:, :, None], axis=1).astype(jnp.bfloat16)


def pipe_bit(level):
    return lax.axis_index("pipe") // (1 << level) % 2 == 1


def regroup(blocks):
    for level in range(GROUP.bit_length() - 1):
        outer = blocks.shape[0] >> level + 1
        inner = 1 << level
        shaped = blocks.reshape((outer, 2, inner) + blocks.shape[1:])
        is_upper = pipe_bit(level)
        lower_half = shaped[:, 0]
        upper_half = shaped[:, 1]
        outgoing = jnp.where(is_upper, lower_half, upper_half)
        incoming = partner(outgoing, "pipe", level)
        restored = jnp.stack(
            [jnp.where(is_upper, incoming, lower_half), jnp.where(is_upper, upper_half, incoming)],
            axis=1,
        )
        blocks = restored.reshape(blocks.shape)
    return blocks


def gather_units(piece):
    joined = piece[None]
    for level in range(GROUP.bit_length() - 1):
        incoming = partner(joined, "pipe", level)
        joined = jnp.where(
            pipe_bit(level),
            jnp.concatenate([incoming, joined], axis=0),
            jnp.concatenate([joined, incoming], axis=0),
        )
    return joined


def sum_units(blocks):
    for level in reversed(range(GROUP.bit_length() - 1)):
        middle = blocks.shape[0] // 2
        lower_half = blocks[:middle]
        upper_half = blocks[middle:]
        is_upper = pipe_bit(level)
        kept = jnp.where(is_upper, upper_half, lower_half)
        outgoing = jnp.where(is_upper, lower_half, upper_half)
        blocks = kept + partner(outgoing, "pipe", level)
    return blocks[0]


def send_rows(rows):
    experts, capacity, model_width = rows.shape
    slice_width = model_width // GROUP
    arrived = lax.all_to_all(rows, "expert", split_axis=0, concat_axis=0, tiled=True)
    blocks = jnp.transpose(arrived.reshape(experts * capacity, GROUP, slice_width), (1, 0, 2))
    return regroup(blocks).reshape(GROUP * experts * capacity, slice_width)


def return_rows(produced_rows, experts, capacity, model_width):
    slice_width = produced_rows.shape[1]
    moved = regroup(produced_rows.reshape(GROUP, experts * capacity, slice_width))
    joined = jnp.transpose(moved, (1, 0, 2)).reshape(experts, capacity, model_width)
    back = lax.all_to_all(joined, "expert", split_axis=0, concat_axis=0, tiled=True)
    return back.reshape(experts * capacity, model_width)


def on_device(
    forward_input,
    forward_route,
    forward_gates,
    backward_cotangent,
    backward_route,
    backward_gates,
    gate_up_weight,
    down_weight,
    saved_projections,
):
    experts = lax.axis_size("expert")
    input_rows = forward_input[0]
    cotangent_rows = backward_cotangent[0]
    route_ahead = forward_route[0]
    route_behind = backward_route[0]
    gates_ahead = forward_gates[0]
    gates_behind = backward_gates[0]
    gate_up_product = gate_up_weight[0, 0]
    down_projected_rows = down_weight[0, 0]
    stashed = saved_projections[0, 0]
    model_width = input_rows.shape[1]
    units = down_projected_rows.shape[0] // GROUP
    slice_width = down_projected_rows.shape[1]
    capacity = stashed.shape[0] // (GROUP * experts)
    w_pair = gate_up_product.reshape(2, GROUP, units, slice_width)
    w_down = down_projected_rows.reshape(GROUP, units, slice_width)
    rank_ahead = rank_slots(route_ahead, experts)
    rank_behind = rank_slots(route_behind, experts)
    sent_ahead = gather_rows(
        input_rows, slot_table(route_ahead, rank_ahead, capacity, experts)
    ).reshape(experts, capacity, model_width)
    rows_all = send_rows(sent_ahead)
    partial_value = jnp.einsum(
        "rd,aghd->garh", rows_all, w_pair, preferred_element_type=jnp.float32
    )
    summed = sum_units(partial_value)
    activated, unused = silu_terms(summed[0])
    hidden_all = gather_units((activated * summed[1]).astype(jnp.bfloat16))
    produced_rows = jnp.einsum(
        "grh,ghd->rd", hidden_all, w_down, preferred_element_type=jnp.float32
    ).astype(jnp.bfloat16)
    back_ahead = return_rows(produced_rows, experts, capacity, model_width)
    section_output = combine_rows(back_ahead, route_ahead * capacity + rank_ahead, gates_ahead)
    sent_behind = gather_rows(
        cotangent_rows, slot_table(route_behind, rank_behind, capacity, experts)
    ).reshape(experts, capacity, model_width)
    grads_all = send_rows(sent_behind)
    grad_part = jnp.einsum("rd,ghd->grh", grads_all, w_down, preferred_element_type=jnp.float32)
    hidden_gradient = sum_units(grad_part)
    gate_pre = stashed[:, :units].astype(jnp.float32)
    up_pre = stashed[:, units:].astype(jnp.float32)
    activated, slope = silu_terms(gate_pre)
    pre_part = jnp.concatenate(
        [hidden_gradient * up_pre * slope, hidden_gradient * activated], axis=-1
    ).astype(jnp.bfloat16)
    pre_all = gather_units(pre_part)
    pre_split = pre_all.reshape(GROUP, pre_all.shape[1], 2, units)
    returned = jnp.einsum(
        "grah,aghd->rd", pre_split, w_pair, preferred_element_type=jnp.float32
    ).astype(jnp.bfloat16)
    back_behind = return_rows(returned, experts, capacity, model_width)
    section_gradient = combine_rows(
        back_behind, route_behind * capacity + rank_behind, gates_behind
    )
    next_input = passed_along(section_output[None], "pipe", GROUP)
    prior_gradient = passed_along(section_gradient[None], "pipe", -GROUP)
    return (next_input, prior_gradient)


def solution(mesh):
    return jax.shard_map(
        on_device,
        mesh=mesh,
        in_specs=(
            P("pipe", "expert", None),
            P("pipe", "expert", None),
            P("pipe", "expert", None),
            P("pipe", "expert", None),
            P("pipe", "expert", None),
            P("pipe", "expert", None),
            P("pipe", "expert", None, None),
            P("pipe", "expert", None, None),
            P("pipe", "expert", None, None),
        ),
        out_specs=(P("pipe", "expert", None), P("pipe", "expert", None)),
        check_vma=False,
    )
```

profile of v0, /device:TPU:1, one launch (start us, length us, event | category | flops | bytes accessed | tf_op | source)
XLA Modules:
  0.0 553.3 jit_solution(10751373382897671049)
XLA Ops:
  5.3 1.2 reshape.440
  6.5 13.4 %all-to-all-start.2 = ((bf16[8,9,4096]{2,1,0:T(8,128)(2,1)}), bf16[8,9,4096]{2,1,0:T(8,128)(2,1)S(1)}, u32[]{:S(2)}, u32[]{:S(2)}) async-start(bf16[8,9,4096]{2,1,0:T(8,128)(2,1)} %reshape.440), calls=%async_computation.2 | async-start | bytes 2097152 | tf_op jit(solution)/shard_map/all_to_all | solution.py:99
  21.3 1.7 gather_fusion
  23.0 2.0 broadcast_select_fusion.1
  25.0 2.3 reshape.434
  27.3 11.6 %all-to-all-done.2 = bf16[8,9,4096]{2,1,0:T(8,128)(2,1)S(1)} async-done(((bf16[8,9,4096]{2,1,0:T(8,128)(2,1)}), bf16[8,9,4096]{2,1,0:T(8,128)(2,1)S(1)}, u32[]{:S(2)}, u32[]{:S(2)}) %all-to-all-start.2) | async-done | bytes 589856 | tf_op jit(solution)/shard_map/all_to_all | solution.py:99
  38.9 4.2 all-to-all-start
  43.1 1.2 reshape.441
  44.3 1.2 copy.109
  46.3 11.8 %collective-permute-start.13 = (bf16[4,1,72,512]{3,2,0,1:T(8,128)(2,1)}, bf16[4,1,72,512]{3,2,0,1:T(8,128)(2,1)}, u32[]{:S(2)}, u32[]{:S(2)}) collective-permute-start(bf16[4,1,72,512]{3,2,0,1:T(8,128)(2,1)} %broadcast_select_fusion.9), channel_id=1, source_target_pairs={{0,8},{8,0},{16,24},{24,16},{32,40},{40,32},{48,56},{56,48},{64,72... | collective-permute-start | bytes 884744 | tf_op jit(solution)/shard_map/ppermute | solution.py:12
  58.1 1.5 reshape.435
  59.9 12.4 %collective-permute-start = (bf16[4,1,72,512]{3,2,0,1:T(8,128)(2,1)S(1)}, bf16[4,1,72,512]{3,2,0,1:T(8,128)(2,1)S(1)}, u32[]{:S(2)}, u32[]{:S(2)}) collective-permute-start(bf16[4,1,72,512]{3,2,0,1:T(8,128)(2,1)S(1)} %broadcast_select_fusion.15), channel_id=1, source_target_pairs={{0,8},{8,0},{16,24},{24,16},{32,40},{40,32},{48,56},{56,48},{64,72... | collective-permute-start | bytes 884744 | tf_op jit(solution)/shard_map/ppermute | solution.py:12
  72.3 1.0 broadcast_select_fusion.8
  73.4 17.4 %collective-permute-start.14 = (bf16[2,2,72,512]{3,2,0,1:T(8,128)(2,1)S(1)}, bf16[2,2,72,512]{3,2,0,1:T(8,128)(2,1)S(1)}, u32[]{:S(2)}, u32[]{:S(2)}) collective-permute-start(bf16[2,2,72,512]{3,2,0,1:T(8,128)(2,1)S(1)} %broadcast_select_fusion.17), channel_id=1, source_target_pairs={{0,16},{8,24},{16,0},{24,8},{32,48},{40,56},{48,32},{56,40},{64,80... | collective-permute-start | bytes 884744 | tf_op jit(solution)/shard_map/ppermute | solution.py:12
  90.9 1.9 collective-permute-start.1
  92.8 5.3 collective-permute-done.14
  98.3 1.9 collective-permute-start.15
  100.2 5.2 collective-permute-done.1
  105.7 2.1 collective-permute-start.2
  107.8 13.9 %collective-permute-done.15 = bf16[1,4,72,512]{3,2,1,0:T(8,128)(2,1)S(1)} collective-permute-done((bf16[1,4,72,512]{3,2,1,0:T(8,128)(2,1)S(1)}, bf16[1,4,72,512]{3,2,1,0:T(8,128)(2,1)S(1)}, u32[]{:S(2)}, u32[]{:S(2)}) %collective-permute-start.15) | collective-permute-done | bytes 294944 | tf_op jit(solution)/shard_map/ppermute | solution.py:12
  122.8 1.9 collective-permute-start.16
  124.7 79.2 %collective-permute-done.2 = bf16[1,4,72,512]{3,2,1,0:T(8,128)(2,1)S(1)} collective-permute-done((bf16[1,4,72,512]{3,2,1,0:T(8,128)(2,1)S(1)}, bf16[1,4,72,512]{3,2,1,0:T(8,128)(2,1)S(1)}, u32[]{:S(2)}, u32[]{:S(2)}) %collective-permute-start.2) | collective-permute-done | bytes 294944 | tf_op jit(solution)/shard_map/ppermute | solution.py:12
  204.0 1.4 convolution_bitcast_fusion
  205.6 1.9 collective-permute-start.3
  207.6 21.5 %collective-permute-done.16 = f32[4,576,128]{2,1,0:T(8,128)S(1)} collective-permute-done((f32[4,576,128]{2,1,0:T(8,128)S(1)}, f32[4,576,128]{2,1,0:T(8,128)S(1)}, u32[]{:S(2)}, u32[]{:S(2)}) %collective-permute-start.16) | collective-permute-done | bytes 1179680 | tf_op jit(solution)/shard_map/ppermute | solution.py:12
  229.4 2.1 collective-permute-start.17
  231.4 61.9 %collective-permute-done.17 = f32[2,576,128]{2,1,0:T(8,128)S(1)} collective-permute-done((f32[2,576,128]{2,1,0:T(8,128)S(1)}, f32[2,576,128]{2,1,0:T(8,128)S(1)}, u32[]{:S(2)}, u32[]{:S(2)}) %collective-permute-start.17) | collective-permute-done | bytes 589856 | tf_op jit(solution)/shard_map/ppermute | solution.py:12
  293.4 2.4 collective-permute-start.18
  295.8 1.2 collective-permute-done.18
  297.8 1.9 collective-permute-start.4
  299.8 2.3 collective-permute-start.19
  302.0 1.2 collective-permute-done.19
  303.4 3.6 collective-permute-start.20
  307.1 32.4 %collective-permute-done.20 = bf16[2,576,256]{2,1,0:T(8,128)(2,1)S(1)} collective-permute-done((bf16[2,576,256]{2,1,0:T(8,128)(2,1)S(1)}, bf16[2,576,256]{2,1,0:T(8,128)(2,1)S(1)}, u32[]{:S(2)}, u32[]{:S(2)}) %collective-permute-start.20) | collective-permute-done | bytes 589856 | tf_op jit(solution)/shard_map/ppermute | solution.py:12
  339.7 1.9 collective-permute-start.21
  341.9 3.1 collective-permute-start.5
  345.4 1.2 collective-permute-done.5
  346.8 2.5 collective-permute-start.6
  349.2 46.4 %collective-permute-done.21 = bf16[4,576,256]{2,1,0:T(8,128)(2,1)S(1)} collective-permute-done((bf16[4,576,256]{2,1,0:T(8,128)(2,1)S(1)}, bf16[4,576,256]{2,1,0:T(8,128)(2,1)S(1)}, u32[]{:S(2)}, u32[]{:S(2)}) %collective-permute-start.21) | collective-permute-done | bytes 1179680 | tf_op jit(solution)/shard_map/ppermute | solution.py:12
  395.8 1.4 fusion.5
  397.3 2.5 collective-permute-start.22
  399.8 1.9 collective-permute-start.7
  401.8 8.5 %collective-permute-done.7 = bf16[2,576,128]{2,1,0:T(8,128)(2,1)S(1)} collective-permute-done((bf16[2,576,128]{2,1,0:T(8,128)(2,1)S(1)}, bf16[2,576,128]{2,1,0:T(8,128)(2,1)S(1)}, u32[]{:S(2)}, u32[]{:S(2)}) %collective-permute-start.7) | collective-permute-done | bytes 294944 | tf_op jit(solution)/shard_map/ppermute | solution.py:12
  410.4 1.9 collective-permute-start.8
  412.4 2.2 collective-permute-start.23
  414.6 16.2 %collective-permute-done.23 = bf16[2,2,72,512]{3,2,0,1:T(8,128)(2,1)S(1)} collective-permute-done((bf16[2,2,72,512]{3,2,0,1:T(8,128)(2,1)S(1)}, bf16[2,2,72,512]{3,2,0,1:T(8,128)(2,1)S(1)}, u32[]{:S(2)}, u32[]{:S(2)}) %collective-permute-start.23) | collective-permute-done | bytes 294944 | tf_op jit(solution)/shard_map/ppermute | solution.py:12
  430.9 10.1 %collective-permute-done.8 = bf16[4,576,128]{2,1,0:T(8,128)(2,1)S(1)} collective-permute-done((bf16[4,576,128]{2,1,0:T(8,128)(2,1)S(1)}, bf16[4,576,128]{2,1,0:T(8,128)(2,1)S(1)}, u32[]{:S(2)}, u32[]{:S(2)}) %collective-permute-start.8) | collective-permute-done | bytes 589856 | tf_op jit(solution)/shard_map/ppermute | solution.py:12
  441.8 2.4 collective-permute-start.9
  444.4 1.9 collective-permute-start.24
  447.2 2.3 collective-permute-start.10
  449.5 10.8 %collective-permute-done.24 = bf16[1,4,72,512]{3,2,1,0:T(8,128)(2,1)S(1)} collective-permute-done((bf16[1,4,72,512]{3,2,1,0:T(8,128)(2,1)S(1)}, bf16[1,4,72,512]{3,2,1,0:T(8,128)(2,1)S(1)}, u32[]{:S(2)}, u32[]{:S(2)}) %collective-permute-start.24) | collective-permute-done | bytes 294944 | tf_op jit(solution)/shard_map/ppermute | solution.py:12
  460.6 1.3 reshape.444
  461.9 3.6 all-to-all-start.3
  465.5 1.1 select_bitcast_fusion.11
  466.8 1.9 collective-permute-start.11
  468.7 35.3 %collective-permute-done.11 = bf16[1,4,72,512]{3,2,1,0:T(8,128)(2,1)S(1)} collective-permute-done((bf16[1,4,72,512]{3,2,1,0:T(8,128)(2,1)S(1)}, bf16[1,4,72,512]{3,2,1,0:T(8,128)(2,1)S(1)}, u32[]{:S(2)}, u32[]{:S(2)}) %collective-permute-start.11) | collective-permute-done | bytes 294944 | tf_op jit(solution)/shard_map/ppermute | solution.py:12
  505.2 2.2 reshape.438
  507.4 6.3 %all-to-all-start.1 = ((bf16[8,9,4096]{2,1,0:T(8,128)(2,1)}), bf16[8,9,4096]{2,1,0:T(8,128)(2,1)}, u32[]{:S(2)}, u32[]{:S(2)}) async-start(bf16[8,9,4096]{2,1,0:T(8,128)(2,1)} %reshape.438), calls=%async_computation.1 | async-start | bytes 2097152 | tf_op jit(solution)/shard_map/all_to_all | solution.py:108
  514.5 1.5 reshape.445
  517.7 5.1 collective-permute-start.25
  522.8 18.5 %all-to-all-done.1 = bf16[8,9,4096]{2,1,0:T(8,128)(2,1)} async-done(((bf16[8,9,4096]{2,1,0:T(8,128)(2,1)}), bf16[8,9,4096]{2,1,0:T(8,128)(2,1)}, u32[]{:S(2)}, u32[]{:S(2)}) %all-to-all-start.1) | async-done | bytes 589856 | tf_op jit(solution)/shard_map/all_to_all | solution.py:108
  541.3 1.5 reshape.439
  544.5 3.2 collective-permute-start.12
  547.8 4.2 collective-permute-done.12
  (153 shorter events, 20.4 us)
Async XLA Ops:
  0.6 203.3 %copy-start = (bf16[1,1,2048,512]{3,2,1,0:T(8,128)(2,1)S(1)}, bf16[1,1,2048,512]{3,2,1,0:T(8,128)(2,1)}, u32[]{:S(2)}) copy-start(bf16[1,1,2048,512]{3,2,1,0:T(8,128)(2,1)} %param.19) | copy-start | bytes 6291460
  0.6 3.6 copy-start.1
  6.5 13.4 %copy-start.7 = (s32[1,16,2]{1,2,0:T(2,128)S(1)}, s32[1,16,2]{1,2,0:T(2,128)}, u32[]{:S(2)}) copy-start(s32[1,16,2]{1,2,0:T(2,128)} %param.14) | copy-start | bytes 388
  6.5 14.8 %copy-start.2 = (bf16[1,16,4096]{2,1,0:T(8,128)(2,1)S(1)}, bf16[1,16,4096]{2,1,0:T(8,128)(2,1)}, u32[]{:S(2)}) copy-start(bf16[1,16,4096]{2,1,0:T(8,128)(2,1)} %param.13) | copy-start | bytes 393220
  6.5 32.4 %all-to-all-start.2 = ((bf16[8,9,4096]{2,1,0:T(8,128)(2,1)}), bf16[8,9,4096]{2,1,0:T(8,128)(2,1)S(1)}, u32[]{:S(2)}, u32[]{:S(2)}) async-start(bf16[8,9,4096]{2,1,0:T(8,128)(2,1)} %reshape.440), calls=%async_computation.2 | async-start | bytes 2097152 | tf_op jit(solution)/shard_map/all_to_all | solution.py:99
  38.9 19.2 %all-to-all-start = ((bf16[8,9,4096]{2,1,0:T(8,128)(2,1)}), bf16[8,9,4096]{2,1,0:T(8,128)(2,1)}, u32[]{:S(2)}, u32[]{:S(2)}) async-start(bf16[8,9,4096]{2,1,0:T(8,128)(2,1)} %reshape.434), calls=%async_computation | async-start | bytes 2097152 | tf_op jit(solution)/shard_map/all_to_all | solution.py:99
  46.3 26.0 %collective-permute-start.13 = (bf16[4,1,72,512]{3,2,0,1:T(8,128)(2,1)}, bf16[4,1,72,512]{3,2,0,1:T(8,128)(2,1)}, u32[]{:S(2)}, u32[]{:S(2)}) collective-permute-start(bf16[4,1,72,512]{3,2,0,1:T(8,128)(2,1)} %broadcast_select_fusion.9), channel_id=1, source_target_pairs={{0,8},{8,0},{16,24},{24,16},{32,40},{40,32},{48,56},{56,48},{64,72... | collective-permute-start | bytes 884744 | tf_op jit(solution)/shard_map/ppermute | solution.py:12
  59.9 30.8 %collective-permute-start = (bf16[4,1,72,512]{3,2,0,1:T(8,128)(2,1)S(1)}, bf16[4,1,72,512]{3,2,0,1:T(8,128)(2,1)S(1)}, u32[]{:S(2)}, u32[]{:S(2)}) collective-permute-start(bf16[4,1,72,512]{3,2,0,1:T(8,128)(2,1)S(1)} %broadcast_select_fusion.15), channel_id=1, source_target_pairs={{0,8},{8,0},{16,24},{24,16},{32,40},{40,32},{48,56},{56,48},{64,72... | collective-permute-start | bytes 884744 | tf_op jit(solution)/shard_map/ppermute | solution.py:12
  73.4 24.7 %collective-permute-start.14 = (bf16[2,2,72,512]{3,2,0,1:T(8,128)(2,1)S(1)}, bf16[2,2,72,512]{3,2,0,1:T(8,128)(2,1)S(1)}, u32[]{:S(2)}, u32[]{:S(2)}) collective-permute-start(bf16[2,2,72,512]{3,2,0,1:T(8,128)(2,1)S(1)} %broadcast_select_fusion.17), channel_id=1, source_target_pairs={{0,16},{8,24},{16,0},{24,8},{32,48},{40,56},{48,32},{56,40},{64,80... | collective-permute-start | bytes 884744 | tf_op jit(solution)/shard_map/ppermute | solution.py:12
  90.9 14.6 %collective-permute-start.1 = (bf16[2,2,72,512]{3,2,0,1:T(8,128)(2,1)S(1)}, bf16[2,2,72,512]{3,2,0,1:T(8,128)(2,1)S(1)}, u32[]{:S(2)}, u32[]{:S(2)}) collective-permute-start(bf16[2,2,72,512]{3,2,0,1:T(8,128)(2,1)S(1)} %broadcast_select_fusion.19), channel_id=1, source_target_pairs={{0,16},{8,24},{16,0},{24,8},{32,48},{40,56},{48,32},{56,40},{64,80... | collective-permute-start | bytes 884744 | tf_op jit(solution)/shard_map/ppermute | solution.py:12
  98.3 23.4 %collective-permute-start.15 = (bf16[1,4,72,512]{3,2,1,0:T(8,128)(2,1)S(1)}, bf16[1,4,72,512]{3,2,1,0:T(8,128)(2,1)S(1)}, u32[]{:S(2)}, u32[]{:S(2)}) collective-permute-start(bf16[1,4,72,512]{3,2,1,0:T(8,128)(2,1)S(1)} %broadcast_select_fusion.21), channel_id=1, source_target_pairs={{0,32},{8,40},{16,48},{24,56},{32,0},{40,8},{48,16},{56,24},{64,96... | collective-permute-start | bytes 884744 | tf_op jit(solution)/shard_map/ppermute | solution.py:12
  105.7 16.1 %copy-start.5 = (bf16[1,1,1024,512]{3,2,1,0:T(8,128)(2,1)S(1)}, bf16[1,1,1024,512]{3,2,1,0:T(8,128)(2,1)}, u32[]{:S(2)}) copy-start(bf16[1,1,1024,512]{3,2,1,0:T(8,128)(2,1)} %param.20) | copy-start | bytes 3145732
  105.7 98.1 %collective-permute-start.2 = (bf16[1,4,72,512]{3,2,1,0:T(8,128)(2,1)S(1)}, bf16[1,4,72,512]{3,2,1,0:T(8,128)(2,1)S(1)}, u32[]{:S(2)}, u32[]{:S(2)}) collective-permute-start(bf16[1,4,72,512]{3,2,1,0:T(8,128)(2,1)S(1)} %broadcast_select_fusion.23), channel_id=1, source_target_pairs={{0,32},{8,40},{16,48},{24,56},{32,0},{40,8},{48,16},{56,24},{64,96... | collective-permute-start | bytes 884744 | tf_op jit(solution)/shard_map/ppermute | solution.py:12
  122.8 106.4 %collective-permute-start.16 = (f32[4,576,128]{2,1,0:T(8,128)S(1)}, f32[4,576,128]{2,1,0:T(8,128)S(1)}, u32[]{:S(2)}, u32[]{:S(2)}) collective-permute-start(f32[4,576,128]{2,1,0:T(8,128)S(1)} %slice_select_fusion.1), channel_id=1, source_target_pairs={{0,32},{8,40},{16,48},{24,56},{32,0},{40,8},{48,16},{56,24},{64,96... | collective-permute-start | bytes 3538952 | tf_op jit(solution)/shard_map/ppermute | solution.py:12
  205.6 91.7 %collective-permute-start.3 = (f32[4,2,576,128]{3,2,0,1:T(8,128)S(1)}, f32[4,2,576,128]{3,2,0,1:T(8,128)S(1)}, u32[]{:S(2)}, u32[]{:S(2)}) collective-permute-start(f32[4,2,576,128]{3,2,0,1:T(8,128)S(1)} %slice_select_fusion), channel_id=1, source_target_pairs={{0,32},{8,40},{16,48},{24,56},{32,0},{40,8},{48,16},{56,24},{64,96... | collective-permute-start | bytes 7077896 | tf_op jit(solution)/shard_map/ppermute | solution.py:12
  229.3 67.7 %copy-start.6 = (bf16[1,1,576,256]{3,2,1,0:T(8,128)(2,1)S(1)}, bf16[1,1,576,256]{3,2,1,0:T(8,128)(2,1)}, u32[]{:S(2)}) copy-start(bf16[1,1,576,256]{3,2,1,0:T(8,128)(2,1)} %param.21) | copy-start | bytes 884740
  229.4 64.0 %collective-permute-start.17 = (f32[2,576,128]{2,1,0:T(8,128)S(1)}, f32[2,576,128]{2,1,0:T(8,128)S(1)}, u32[]{:S(2)}, u32[]{:S(2)}) collective-permute-start(f32[2,576,128]{2,1,0:T(8,128)S(1)} %slice_select_fusion.3), channel_id=1, source_target_pairs={{0,16},{8,24},{16,0},{24,8},{32,48},{40,56},{48,32},{56,40},{64,80... | collective-permute-start | bytes 1769480 | tf_op jit(solution)/shard_map/ppermute | solution.py:12
  293.4 3.6 collective-permute-start.18
  297.8 43.8 %collective-permute-start.4 = (f32[2,2,576,128]{3,2,0,1:T(8,128)S(1)}, f32[2,2,576,128]{3,2,0,1:T(8,128)S(1)}, u32[]{:S(2)}, u32[]{:S(2)}) collective-permute-start(f32[2,2,576,128]{3,2,0,1:T(8,128)S(1)} %slice_select_fusion.2), channel_id=1, source_target_pairs={{0,16},{8,24},{16,0},{24,8},{32,48},{40,56},{48,32},{56,40},{64,80... | collective-permute-start | bytes 3538952 | tf_op jit(solution)/shard_map/ppermute | solution.py:12
  299.8 3.5 collective-permute-start.19
  303.4 36.1 %collective-permute-start.20 = (bf16[2,576,256]{2,1,0:T(8,128)(2,1)S(1)}, bf16[2,576,256]{2,1,0:T(8,128)(2,1)S(1)}, u32[]{:S(2)}, u32[]{:S(2)}) collective-permute-start(bf16[2,576,256]{2,1,0:T(8,128)(2,1)S(1)} %maximum_select_fusion.6), channel_id=1, source_target_pairs={{0,16},{8,24},{16,0},{24,8},{32,48},{40,56},{48,32},{56,40},{64,80... | collective-permute-start | bytes 1769480 | tf_op jit(solution)/shard_map/ppermute | solution.py:12
  339.7 55.9 %collective-permute-start.21 = (bf16[4,576,256]{2,1,0:T(8,128)(2,1)S(1)}, bf16[4,576,256]{2,1,0:T(8,128)(2,1)S(1)}, u32[]{:S(2)}, u32[]{:S(2)}) collective-permute-start(bf16[4,576,256]{2,1,0:T(8,128)(2,1)S(1)} %maximum_select_fusion.3), channel_id=1, source_target_pairs={{0,32},{8,40},{16,48},{24,56},{32,0},{40,8},{48,16},{56,24},{64,96... | collective-permute-start | bytes 3538952 | tf_op jit(solution)/shard_map/ppermute | solution.py:12
  341.9 4.7 collective-permute-start.5
  346.8 53.0 %collective-permute-start.6 = (bf16[1,576,128]{2,1,0:T(8,128)(2,1)S(1)}, bf16[1,576,128]{2,1,0:T(8,128)(2,1)S(1)}, u32[]{:S(2)}, u32[]{:S(2)}) collective-permute-start(bf16[1,576,128]{2,1,0:T(8,128)(2,1)S(1)} %fusion.36), channel_id=1, source_target_pairs={{0,8},{8,0},{16,24},{24,16},{32,40},{40,32},{48,56},{56,48},{64,72... | collective-permute-start | bytes 442376 | tf_op jit(solution)/shard_map/ppermute | solution.py:12
  397.3 4.4 collective-permute-start.22
  399.8 10.5 %collective-permute-start.7 = (bf16[2,576,128]{2,1,0:T(8,128)(2,1)S(1)}, bf16[2,576,128]{2,1,0:T(8,128)(2,1)S(1)}, u32[]{:S(2)}, u32[]{:S(2)}) collective-permute-start(bf16[2,576,128]{2,1,0:T(8,128)(2,1)S(1)} %maximum_select_fusion.8), channel_id=1, source_target_pairs={{0,16},{8,24},{16,0},{24,8},{32,48},{40,56},{48,32},{56,40},{64,80... | collective-permute-start | bytes 884744 | tf_op jit(solution)/shard_map/ppermute | solution.py:12
  410.4 30.6 %collective-permute-start.8 = (bf16[4,576,128]{2,1,0:T(8,128)(2,1)S(1)}, bf16[4,576,128]{2,1,0:T(8,128)(2,1)S(1)}, u32[]{:S(2)}, u32[]{:S(2)}) collective-permute-start(bf16[4,576,128]{2,1,0:T(8,128)(2,1)S(1)} %maximum_select_fusion.5), channel_id=1, source_target_pairs={{0,32},{8,40},{16,48},{24,56},{32,0},{40,8},{48,16},{56,24},{64,96... | collective-permute-start | bytes 1769480 | tf_op jit(solution)/shard_map/ppermute | solution.py:12
  412.4 18.5 %collective-permute-start.23 = (bf16[2,2,72,512]{3,2,0,1:T(8,128)(2,1)S(1)}, bf16[2,2,72,512]{3,2,0,1:T(8,128)(2,1)S(1)}, u32[]{:S(2)}, u32[]{:S(2)}) collective-permute-start(bf16[2,2,72,512]{3,2,0,1:T(8,128)(2,1)S(1)} %broadcast_select_fusion.16), channel_id=1, source_target_pairs={{0,16},{8,24},{16,0},{24,8},{32,48},{40,56},{48,32},{56,40},{64,80... | collective-permute-start | bytes 884744 | tf_op jit(solution)/shard_map/ppermute | solution.py:12
  441.8 4.5 collective-permute-start.9
  444.4 15.9 %collective-permute-start.24 = (bf16[1,4,72,512]{3,2,1,0:T(8,128)(2,1)S(1)}, bf16[1,4,72,512]{3,2,1,0:T(8,128)(2,1)S(1)}, u32[]{:S(2)}, u32[]{:S(2)}) collective-permute-start(bf16[1,4,72,512]{3,2,1,0:T(8,128)(2,1)S(1)} %broadcast_select_fusion.20), channel_id=1, source_target_pairs={{0,32},{8,40},{16,48},{24,56},{32,0},{40,8},{48,16},{56,24},{64,96... | collective-permute-start | bytes 884744 | tf_op jit(solution)/shard_map/ppermute | solution.py:12
  446.4 14.0 %copy-start.4 = (bf16[4,1,72,512]{3,2,0,1:T(8,128)(2,1)}, bf16[4,1,72,512]{3,2,0,1:T(8,128)(2,1)S(1)}, u32[]{:S(2)}) copy-start(bf16[4,1,72,512]{3,2,0,1:T(8,128)(2,1)S(1)} %get-tuple-element.27) | copy-start | bytes 884740
  447.2 18.3 %collective-permute-start.10 = (bf16[2,2,72,512]{3,2,0,1:T(8,128)(2,1)}, bf16[2,2,72,512]{3,2,0,1:T(8,128)(2,1)}, u32[]{:S(2)}, u32[]{:S(2)}) collective-permute-start(bf16[2,2,72,512]{3,2,0,1:T(8,128)(2,1)} %broadcast_select_fusion.18), channel_id=1, source_target_pairs={{0,16},{8,24},{16,0},{24,8},{32,48},{40,56},{48,32},{56,40},{64,80... | collective-permute-start | bytes 884744 | tf_op jit(solution)/shard_map/ppermute | solution.py:12
  461.9 45.5 %all-to-all-start.3 = ((bf16[8,9,4096]{2,1,0:T(8,128)(2,1)}), bf16[8,9,4096]{2,1,0:T(8,128)(2,1)S(1)}, u32[]{:S(2)}, u32[]{:S(2)}) async-start(bf16[8,9,4096]{2,1,0:T(8,128)(2,1)} %reshape.444), calls=%async_computation.3 | async-start | bytes 2097152 | tf_op jit(solution)/shard_map/all_to_all | solution.py:108
  466.8 37.2 %collective-permute-start.11 = (bf16[1,4,72,512]{3,2,1,0:T(8,128)(2,1)S(1)}, bf16[1,4,72,512]{3,2,1,0:T(8,128)(2,1)S(1)}, u32[]{:S(2)}, u32[]{:S(2)}) collective-permute-start(bf16[1,4,72,512]{3,2,1,0:T(8,128)(2,1)S(1)} %broadcast_select_fusion.22), channel_id=1, source_target_pairs={{0,32},{8,40},{16,48},{24,56},{32,0},{40,8},{48,16},{56,24},{64,96... | collective-permute-start | bytes 884744 | tf_op jit(solution)/shard_map/ppermute | solution.py:12
  507.4 6.6 %copy-start.9 = (f32[1,16,2]{1,2,0:T(2,128)S(1)}, f32[1,16,2]{1,2,0:T(2,128)}, u32[]{:S(2)}) copy-start(f32[1,16,2]{1,2,0:T(2,128)} %param.15) | copy-start | bytes 388
  507.4 6.7 %copy-start.8 = (s32[1,16,2]{1,2,0:T(2,128)S(1)}, s32[1,16,2]{1,2,0:T(2,128)}, u32[]{:S(2)}) copy-start(s32[1,16,2]{1,2,0:T(2,128)} %param.17) | copy-start | bytes 388
  507.4 7.0 %copy-start.10 = (f32[1,16,2]{1,2,0:T(2,128)S(1)}, f32[1,16,2]{1,2,0:T(2,128)}, u32[]{:S(2)}) copy-start(f32[1,16,2]{1,2,0:T(2,128)} %param.18) | copy-start | bytes 388
  507.4 7.1 %copy-start.3 = (bf16[8,9,4096]{2,1,0:T(8,128)(2,1)}, bf16[8,9,4096]{2,1,0:T(8,128)(2,1)S(1)}, u32[]{:S(2)}) copy-start(bf16[8,9,4096]{2,1,0:T(8,128)(2,1)S(1)} %all-to-all-done.3) | copy-start | bytes 1769476
  507.4 33.9 %all-to-all-start.1 = ((bf16[8,9,4096]{2,1,0:T(8,128)(2,1)}), bf16[8,9,4096]{2,1,0:T(8,128)(2,1)}, u32[]{:S(2)}, u32[]{:S(2)}) async-start(bf16[8,9,4096]{2,1,0:T(8,128)(2,1)} %reshape.438), calls=%async_computation.1 | async-start | bytes 2097152 | tf_op jit(solution)/shard_map/all_to_all | solution.py:108
  517.7 30.0 %collective-permute-start.25 = (bf16[1,16,4096]{2,1,0:T(8,128)(2,1)S(1)}, bf16[1,16,4096]{2,1,0:T(8,128)(2,1)S(1)}, u32[]{:S(2)}, u32[]{:S(2)}) collective-permute-start(bf16[1,16,4096]{2,1,0:T(8,128)(2,1)S(1)} %bitcast.375), channel_id=1, source_target_pairs={{0,448},{8,456},{16,464},{24,472},{32,480},{40,488},{48,496},{56,5... | collective-permute-start | bytes 393224 | tf_op jit(solution)/shard_map/ppermute | solution.py:17
  544.5 7.4 %collective-permute-start.12 = (bf16[1,16,4096]{2,1,0:T(8,128)(2,1)S(1)}, bf16[1,16,4096]{2,1,0:T(8,128)(2,1)S(1)}, u32[]{:S(2)}, u32[]{:S(2)}) collective-permute-start(bf16[1,16,4096]{2,1,0:T(8,128)(2,1)S(1)} %bitcast.376), channel_id=1, source_target_pairs={{0,64},{8,72},{16,80},{24,88},{32,96},{40,104},{48,112},{56,120},{... | collective-permute-start | bytes 393224 | tf_op jit(solution)/shard_map/ppermute | solution.py:17
where the time goes:
time: 555 us; the launch traced here: 553 us
  waiting for transfers between devices  385 us (69%)
  starting transfers between devices  124 us (22%)
  local copies, waits for them, and re-layouts  24.7 us (4%)
  other arithmetic  14 us (3%)
    ppermute x24, waiting for transfers between devices, partner(): return lax.ppermute(value, axis, pairs)  350 us
    ppermute x24, starting transfers between devices, partner(): return lax.ppermute(value, axis, pairs)  88.1 us
    all_to_all x2, waiting for transfers between devices, return_rows(): lax.all_to_all(joined, 'expert', split_axis=0, concat_axis=0, tiled=True)  18.5 us
    all_to_all x2, starting transfers between devices, send_rows(): lax.all_to_all(rows, 'expert', split_axis=0, concat_axis=0, tiled=True)  17.7 us
    all_to_all x2, waiting for transfers between devices, send_rows(): lax.all_to_all(rows, 'expert', split_axis=0, concat_axis=0, tiled=True)  11.6 us
  transfers between devices with their start and end apart: 30, of which 19 were waited for; matrix products, arithmetic and copies ran while one was open for 6% of the time, Pallas kernels for 0%

commit v1 on v0

v1 whole, which is shorter than its diff:
```python
import functools

import jax
import jax.numpy as jnp
import numpy as np
from jax import lax
from jax.experimental import pallas as pl
from jax.experimental.pallas import tpu as pltpu
from jax.sharding import PartitionSpec as P

GROUP = 8
BASE = 4
OVER = 5
ZN = 16
XN = 4
LINE = 4
CHUNK = ZN * (BASE + OVER)
MESH = pl.DeviceIdType.MESH


def permutations():
    norm_out = np.zeros((256, 256), np.float32)
    over_out = np.zeros((2, 80, 256), np.float32)
    norm_back = np.zeros((256, XN * CHUNK), np.float32)
    over_back = np.zeros((2, 256, XN * CHUNK), np.float32)
    stash = np.zeros((XN * CHUNK, XN * CHUNK), np.float32)
    for g in range(ZN):
        for x in range(XN):
            for s in range(BASE):
                norm_out[x * 64 + g * 4 + s, g * 16 + x * 4 + s] = 1
                norm_back[g * 16 + x * 4 + s, x * CHUNK + g * 4 + s] = 1
                source = (g % 8) * 8 + x * 2 + g // 8
                stash[x * CHUNK + g * 4 + s, source * 9 + s] = 1
            for j in range(OVER):
                for half in range(2):
                    over_out[half, g * 5 + j, g * 16 + half * 8 + j] = 1
                    over_back[half, g * 16 + half * 8 + j, x * CHUNK + 64 + g * 5 + j] = 1
                stash[x * CHUNK + 64 + g * 5 + j, source * 9 + 4 + j] = 1
    return [a.astype(jnp.bfloat16) for a in (norm_out, over_out, norm_back, over_back, stash)]


def dot(a, b):
    return jnp.dot(a, b, preferred_element_type=jnp.float32)


def dot_t(a, b):
    return lax.dot_general(a, b, (((1,), (1,)), ((), ())), preferred_element_type=jnp.float32)


def sigmoid(v):
    return 1.0 / (1.0 + jnp.exp(-v))


def route_ranks(route):
    lane = lax.broadcasted_iota(jnp.int32, (16, 128), 1)
    first = route[:, 0:1]
    second = route[:, 1:2]
    hits = jnp.where(first == lane, 1.0, 0.0) + jnp.where(second == lane, 1.0, 0.0)
    row = lax.broadcasted_iota(jnp.int32, (16, 16), 0)
    col = lax.broadcasted_iota(jnp.int32, (16, 16), 1)
    earlier = jnp.where(col < row, 1.0, 0.0).astype(jnp.bfloat16)
    before = dot(earlier, hits.astype(jnp.bfloat16))
    ranks = []
    for pick in (first, second):
        rank = jnp.sum(jnp.where(pick == lane, before, 0.0), axis=1, keepdims=True)
        ranks.append(rank.astype(jnp.int32))
    return ranks, jnp.sum(hits, axis=0, keepdims=True)


def choice_match(route, ranks, half=None):
    col = lax.broadcasted_iota(jnp.int32, (16, 128), 1)
    is_norm = col < 32
    expert = ((col >> 2) & 3) * 2 + (col >> 4)
    slot = jnp.where(is_norm, col & 3, 4 + (col & 7))
    if half is not None:
        slot = jnp.where(is_norm | (((col >> 3) & 1) == half), slot, 99)
    slot = jnp.where(col < (48 if half is None else 64), slot, 99)
    out = []
    for k in range(2):
        pick = route[:, k : k + 1]
        out.append((slot == ranks[k]) & ((expert == pick) | jnp.logical_not(is_norm)))
    return out


def gate_parts(route, gates, ranks, half):
    match = choice_match(route, ranks, half)
    total = jnp.where(match[0], gates[:, 0:1], 0.0) + jnp.where(match[1], gates[:, 1:2], 0.0)
    total = total[:, :64]
    high = total.astype(jnp.bfloat16)
    rest = total - high.astype(jnp.float32)
    middle = rest.astype(jnp.bfloat16)
    low = (rest - middle.astype(jnp.float32)).astype(jnp.bfloat16)
    return jnp.concatenate([high, middle, low], axis=0)


def kernel(
    x_f, r_f, g_f, x_b, r_b, g_b, wgu_h, wd_h, saved_h, p_no, p_oo, p_nb, p_ob, p_st,
    out_f, out_b,
    wgu, wd, wgu_s, wd_s, saved, c_no, c_oo, c_nb, c_ob, c_st,
    zsend, zrecv, xsend, xrecv, xsib,
    own_f, own_b, rss_f, rss_b, rsr_f, rsr_b, hid, pre,
    oret, orecv, wsend, wrecv, comb,
    load_sem, wx_ss, wx_rs, z_ss, z_rs, x_ss, x_rs, c_ss, c_rs, rs_ss, rs_rs, ag_ss, ag_rs, as_ss, as_rs,
    o_ss, o_rs, w_ss, w_rs, y_ss, y_rs,
):
    pipe = lax.axis_index("pipe")
    expert = lax.axis_index("expert")
    y, h = pipe // 8, pipe % 8
    zl, core = h // 2, h % 2
    x, zh = expert // 2, expert % 2
    g = zh * 8 + h

    def ring_id(gg):
        return (y * 8 + gg % 8, x * 2 + gg // 8)

    def x_id(xx):
        return (pipe, xx * 2 + zh)

    def line_id(zz):
        return (y * 8 + zz * 2 + core, expert)

    sib_id = (pipe + 1 - 2 * core, expert)

    def remote(src, dst, ss, rs, dev):
        return pltpu.make_async_remote_copy(
            src_ref=src, dst_ref=dst, send_sem=ss, recv_sem=rs, device_id=dev, device_id_type=MESH
        )

    loads = [
        pltpu.make_async_copy(a, b, load_sem.at[i])
        for i, (a, b) in enumerate(
            ((p_no, c_no), (p_oo, c_oo), (wgu_h, wgu), (wd_h, wd), (saved_h, saved), (p_st, c_st), (p_nb, c_nb), (p_ob, c_ob))
        )
    ]
    for load in loads:
        load.start()

    barrier = pltpu.get_barrier_semaphore()
    peers = [ring_id((g + d) % ZN) for d in range(1, ZN)]
    peers += [x_id((x + d) % XN) for d in range(1, XN)]
    peers += [((pipe + 8) % 64, expert), ((pipe + 56) % 64, expert)]
    for peer in peers:
        pl.semaphore_signal(barrier, inc=1, device_id=peer, device_id_type=MESH)

    routing = []
    for t, (xin, r_ref) in enumerate(((x_f, r_f), (x_b, r_b))):
        route = r_ref[...]
        ranks, counts = route_ranks(route)
        match = choice_match(route, ranks)
        pick = jnp.where(match[0] | match[1], 1.0, 0.0)
        pick = jnp.concatenate([pick, jnp.zeros((112, 128), jnp.float32)], axis=0)
        pick = jnp.transpose(pick)[:48, :16].astype(jnp.bfloat16)
        lane = lax.broadcasted_iota(jnp.int32, (1, 128), 1)
        mine = jnp.sum(jnp.where(lane == expert, counts, 0.0), axis=1, keepdims=True)
        routing.append((route, ranks, mine))
        upper = lax.broadcasted_iota(jnp.int32, (16, 256), 0) < 8
        for b in range(8):
            rows = dot(pick, xin[:, b * 512 : (b + 1) * 512]).astype(jnp.float32)
            over = jnp.where(upper, rows[32:48, :256], rows[32:48, 256:]).astype(jnp.bfloat16)
            for hi in range(2):
                zsend[t, hi * 8 + b, :, 0:512] = rows[hi * 16 : hi * 16 + 16].astype(jnp.bfloat16)
                zsend[t, hi * 8 + b, :, 512:768] = over

    pl.semaphore_wait(barrier, len(peers))

    def z_copy(t, d):
        to = (g + d) % ZN
        return remote(zsend.at[t, to], zrecv.at[t, g], z_ss.at[t, d], z_rs.at[t, d], ring_id(to))

    for t in range(2):
        for d in range(1, ZN):
            z_copy(t, d).start()
        zrecv[t, g] = zsend[t, g]

    wx = [
        remote(wgu_h.at[:, :, 1 - core], wgu_s, wx_ss.at[0], wx_rs.at[0], sib_id),
        remote(wd_h.at[:, 1 - core], wd_s, wx_ss.at[1], wx_rs.at[1], sib_id),
    ]
    for copy in wx:
        copy.start()
    loads[0].wait()
    loads[1].wait()

    def x_copy(t, d):
        to = (x + d) % XN
        return remote(xsend.at[t, to], xrecv.at[t, x], x_ss.at[t, d], x_rs.at[t, d], x_id(to))

    def chunk_of(i):
        return (x + XN - i) % XN

    def c_copy(t, i):
        at = chunk_of(i)
        return remote(xrecv.at[t, at], xsib.at[t, at], c_ss.at[t, i], c_rs.at[t, i], sib_id)

    for t in range(2):
        for d in range(1, ZN):
            z_copy(t, d).wait_recv()
        got = zrecv[t].reshape(256, 768)
        norm = dot(c_no[...], got[:, :512]).astype(jnp.bfloat16)
        over = jnp.concatenate(
            [dot(c_oo[0], got[:, 512:]), dot(c_oo[1], got[:, 512:])], axis=1
        ).astype(jnp.bfloat16)
        for xx in range(XN):
            xsend[t, xx, 0:64] = norm[xx * 64 : xx * 64 + 64]
            xsend[t, xx, 64:CHUNK] = over
        for d in range(1, XN):
            x_copy(t, d).start()
        xrecv[t, x] = xsend[t, x]
        c_copy(t, 0).start()

    for i in range(1, XN):
        for t in range(2):
            x_copy(t, i).wait_recv()
            c_copy(t, i).start()

    for load in loads[2:]:
        load.wait()
    for copy in wx:
        copy.wait_recv()

    rss = (rss_f, rss_b)
    rsr = (rsr_f, rsr_b)
    owns = (own_f, own_b)

    def rs_copy(t, d, i):
        return remote(
            rss[t].at[i, d], rsr[t].at[i, d], rs_ss.at[t, i, d], rs_rs.at[t, i, d], line_id((zl + d) % LINE)
        )

    for i in range(XN):
        at = chunk_of(i)
        for t in range(2):
            c_copy(t, i).wait_recv()
            mine = xrecv[t, at]
            other = xsib[t, at]
            for d in (2, 1, 3, 0):
                to = (zl + d) % LINE
                if t == 0:
                    w_mine = jnp.concatenate([wgu[0, to, core], wgu[1, to, core]], axis=0)
                    w_other = jnp.concatenate([wgu_s[0, to], wgu_s[1, to]], axis=0)
                else:
                    w_mine = wd[to, core]
                    w_other = wd_s[to]
                part = dot_t(mine, w_mine) + dot_t(other, w_other)
                if d == 0:
                    owns[t][i] = part
                else:
                    rss[t][i, d] = part.astype(jnp.bfloat16)
                    rs_copy(t, d, i).start()

    full = (hid, pre)

    def lanes(block):
        return pl.ds(pl.multiple_of(block * 128, 128), 128)

    def ag_copy(t, d, i):
        here = full[t].at[i, :, :, lanes(h)]
        return remote(here, here, ag_ss.at[t, i, d], ag_rs.at[t, i, d], line_id((zl + d) % LINE))

    def as_copy(t, d, i):
        block = ((zl + LINE - d) % LINE) * 2 + core
        here = full[t].at[i, :, :, lanes(block)]
        return remote(here, here, as_ss.at[t, i, d], as_rs.at[t, i, d], sib_id)

    for i in range(XN):
        at = chunk_of(i)
        for t in range(2):
            total = owns[t][i]
            for d in range(1, LINE):
                rs_copy(t, d, i).wait_recv()
                total = total + rsr[t][i, d].astype(jnp.float32)
            if t == 0:
                gate, up = total[:, :128], total[:, 128:]
                hid[i, 0, :, lanes(h)] = (gate * sigmoid(gate) * up).astype(jnp.bfloat16)
            else:
                kept = dot(c_st[pl.ds(pl.multiple_of(at * CHUNK, CHUNK), CHUNK), :], saved[...])
                gate, up = kept[:, :128], kept[:, 128:]
                sig = sigmoid(gate)
                pre[i, 0, :, lanes(h)] = (total * up * (sig * (1.0 + gate * (1.0 - sig)))).astype(jnp.bfloat16)
                pre[i, 1, :, lanes(h)] = (total * (gate * sig)).astype(jnp.bfloat16)
            for d in (2, 1, 3):
                ag_copy(t, d, i).start()
            as_copy(t, 0, i).start()

    for i in range(XN):
        for t in range(2):
            for d in range(1, LINE):
                ag_copy(t, d, i).wait_recv()
                as_copy(t, d, i).start()

    def o_copy(t, i):
        to = chunk_of(i)
        return remote(oret.at[t, to], orecv.at[t, x], o_ss.at[t, i], o_rs.at[t, i], x_id(to))

    wgu_flat = wgu.reshape(2, 1024, 512)
    wd_flat = wd.reshape(1024, 512)
    row = lax.broadcasted_iota(jnp.int32, (CHUNK, 512), 0)
    for i in (1, 2, 3, 0):
        at = chunk_of(i)
        for t in range(2):
            for d in range(LINE):
                as_copy(t, d, i).wait_recv()
            if t == 0:
                made = dot(hid[i, 0], wd_flat[...])
            else:
                made = dot(pre[i, 0], wgu_flat[0]) + dot(pre[i, 1], wgu_flat[1])
            made = jnp.where((row < 64) | (routing[t][2] > 4.5), made, 0.0).astype(jnp.bfloat16)
            if i == 0:
                orecv[t, x] = made
            else:
                oret[t, at] = made
                o_copy(t, i).start()

    def w_copy(t, d):
        to = (g + d) % ZN
        return remote(wsend.at[t, to], wrecv.at[t, g], w_ss.at[t, d], w_rs.at[t, d], ring_id(to))

    for t in range(2):
        for i in range(1, XN):
            o_copy(t, i).wait_recv()
        got = orecv[t].reshape(XN * CHUNK, 512)
        wsend[t, :, :, 0:512] = dot(c_nb[...], got).astype(jnp.bfloat16).reshape(ZN, 16, 512)
        over = dot(c_ob[0], got[:, :256]) + dot(c_ob[1], got[:, 256:])
        wsend[t, :, :, 512:768] = over.astype(jnp.bfloat16).reshape(ZN, 16, 256)
        for d in range(1, ZN):
            w_copy(t, d).start()
        wrecv[t, g] = wsend[t, g]

    ends = (((pipe + 8) % 64, expert), ((pipe + 56) % 64, expert))
    outs = (out_f, out_b)

    def y_copy(t):
        return remote(comb.at[t], outs[t], y_ss.at[t], y_rs.at[t], ends[t])

    for t, gates in enumerate((g_f, g_b)):
        route, ranks, _ = routing[t]
        parts = [gate_parts(route, gates[...], ranks, half) for half in range(2)]
        for d in range(1, ZN):
            w_copy(t, d).wait_recv()
        for b in range(8):
            for half in range(2):
                lo = half * 256
                rows = jnp.concatenate(
                    [
                        wrecv[t, b, :, lo : lo + 256],
                        wrecv[t, 8 + b, :, lo : lo + 256],
                        wrecv[t, b, :, 512:768],
                        wrecv[t, 8 + b, :, 512:768],
                    ],
                    axis=0,
                )
                mixed = dot(parts[half], rows)
                mixed = mixed[0:16] + mixed[16:32] + mixed[32:48]
                comb[t, :, b * 512 + lo : b * 512 + lo + 256] = mixed.astype(jnp.bfloat16)
        y_copy(t).start()

    for copy in wx:
        copy.wait_send()
    for t in range(2):
        for d in range(1, ZN):
            z_copy(t, d).wait_send()
            w_copy(t, d).wait_send()
        for d in range(1, XN):
            x_copy(t, d).wait_send()
            o_copy(t, d).wait_send()
        for i in range(XN):
            c_copy(t, i).wait_send()
            as_copy(t, 0, i).wait_send()
            for d in range(1, LINE):
                rs_copy(t, d, i).wait_send()
                ag_copy(t, d, i).wait_send()
                as_copy(t, d, i).wait_send()
    for t in range(2):
        y_copy(t).wait()


def on_device(x_f, r_f, g_f, x_b, r_b, g_b, gate_up, down, saved):
    vmem = pl.BlockSpec(memory_space=pltpu.VMEM)
    anywhere = pl.BlockSpec(memory_space=pl.ANY)
    bf16, f32 = jnp.bfloat16, jnp.float32
    dma = pltpu.SemaphoreType.DMA
    consts = [jnp.asarray(a) for a in permutations()]
    out = jax.ShapeDtypeStruct((16, 4096), bf16)
    scratch = [
        pltpu.VMEM((2, 4, 2, 128, 512), bf16),
        pltpu.VMEM((4, 2, 128, 512), bf16),
        pltpu.VMEM((2, 4, 128, 512), bf16),
        pltpu.VMEM((4, 128, 512), bf16),
        pltpu.VMEM((576, 256), bf16),
    ]
    scratch += [pltpu.VMEM(c.shape, bf16) for c in consts]
    scratch += [
        pltpu.VMEM((2, ZN, 16, 768), bf16),
        pltpu.VMEM((2, ZN, 16, 768), bf16),
        pltpu.VMEM((2, XN, CHUNK, 512), bf16),
        pltpu.VMEM((2, XN, CHUNK, 512), bf16),
        pltpu.VMEM((2, XN, CHUNK, 512), bf16),
        pltpu.VMEM((XN, CHUNK, 256), f32),
        pltpu.VMEM((XN, CHUNK, 128), f32),
        pltpu.VMEM((XN, LINE, CHUNK, 256), bf16),
        pltpu.VMEM((XN, LINE, CHUNK, 128), bf16),
        pltpu.VMEM((XN, LINE, CHUNK, 256), bf16),
        pltpu.VMEM((XN, LINE, CHUNK, 128), bf16),
        pltpu.VMEM((XN, 1, CHUNK, 1024), bf16),
        pltpu.VMEM((XN, 2, CHUNK, 1024), bf16),
        pltpu.VMEM((2, XN, CHUNK, 512), bf16),
        pltpu.VMEM((2, XN, CHUNK, 512), bf16),
        pltpu.VMEM((2, ZN, 16, 768), bf16),
        pltpu.VMEM((2, ZN, 16, 768), bf16),
        pltpu.VMEM((2, 16, 4096), bf16),
    ]
    scratch += [dma((8,)), dma((2,)), dma((2,))]
    scratch += [dma((2, ZN)), dma((2, ZN)), dma((2, XN)), dma((2, XN)), dma((2, XN)), dma((2, XN))]
    scratch += [dma((2, XN, LINE))] * 6
    scratch += [dma((2, XN)), dma((2, XN)), dma((2, ZN)), dma((2, ZN)), dma((2,)), dma((2,))]
    call = pl.pallas_call(
        kernel,
        out_shape=[out, out],
        in_specs=[vmem] * 6 + [anywhere] * 8,
        out_specs=[anywhere, anywhere],
        scratch_shapes=scratch,
        compiler_params=pltpu.CompilerParams(
            collective_id=0, has_side_effects=True, vmem_limit_bytes=48 * 1024 * 1024
        ),
        cost_estimate=pl.CostEstimate(flops=4 * 10**9, bytes_accessed=8 * 10**6, transcendentals=10**6),
    )
    next_input, prior_gradient = call(
        x_f[0], r_f[0], g_f[0], x_b[0], r_b[0], g_b[0],
        gate_up.reshape(2, 4, 2, 128, 512), down.reshape(4, 2, 128, 512), saved[0, 0], *consts,
    )
    return next_input[None], prior_gradient[None]


def solution(mesh):
    row = P("pipe", "expert", None)
    wide = P("pipe", "expert", None, None)
    return jax.shard_map(
        on_device,
        mesh=mesh,
        in_specs=(row,) * 6 + (wide,) * 3,
        out_specs=(row, row),
        check_vma=False,
    )
```

time: 555 us -> 179 us (0.32)
  waiting for transfers between devices: 385 us -> 0 us
  Pallas kernels: 0 us -> 163 us
  starting transfers between devices: 124 us -> 0 us
  other arithmetic: 14 us -> 0 us
  local copies, waits for them, and re-layouts: 24.7 us -> 14.9 us
    ppermute x26 -> x0, waiting for transfers between devices: 354 us -> none  [the longest x24 350 us: partner(): return lax.ppermute(value, axis, pairs)]
    pallas_call x0 -> x1, Pallas kernels: none -> 163 us  [on_device(): call(x_f[0], r_f[0], g_f[0], x_b[0], r_b[0], g_b[0], gate_up.reshape(2, 4...]
    ppermute x26 -> x0, starting transfers between devices: 96.4 us -> none  [the longest x24 88.1 us: partner(): return lax.ppermute(value, axis, pairs)]
    all_to_all x4 -> x0, waiting for transfers between devices: 30.1 us -> none  [the longest x2 18.5 us: return_rows(): lax.all_to_all(joined, 'expert', split_axis=0, concat_axis=0, tiled=True)]
    all_to_all x4 -> x0, starting transfers between devices: 27.5 us -> none  [the longest x2 17.7 us: send_rows(): lax.all_to_all(rows, 'expert', split_axis=0, concat_axis=0, tiled=True)]
    reshape x11 -> x0, local copies, waits for them, and re-layouts: 14 us -> none  [the longest x2 3.54 us: return_rows(): jnp.transpose(moved, (1, 0, 2)).reshape(experts, capacity, model_width)]
    unnamed x24 -> x22, local copies, waits for them, and re-layouts: 1.36 us -> 11.9 us
    select_n x34 -> x0, other arithmetic: 6.64 us -> none  [the longest x4 2.12 us: gather_rows(): return jnp.take(values, source_rows, axis=0, mode='fill', fill_value=0)]
  transfers between devices with their start and end apart: 30 -> 0, of which waited for: 19 -> 0; matrix products, arithmetic and copies ran while one was open for 6% -> 0% of each run, Pallas kernels for 0% -> 0%
where the time goes in v1:
time: 179 us; the launch traced here: 178 us
  Pallas kernels  163 us (91%)
  local copies, waits for them, and re-layouts  14.9 us (8%)
    pallas_call x1, Pallas kernels, on_device(): call(x_f[0], r_f[0], g_f[0], x_b[0], r_b[0], g_b[0], gate_up.reshape(2, 4...  163 us
    unnamed x22, local copies, waits for them, and re-layouts  11.9 us

profile of v1, /device:TPU:1, one launch (start us, length us, event | category | flops | bytes accessed | tf_op | source)
XLA Modules:
  0.0 178.1 jit_solution(11569789271737942568)
XLA Ops:
  0.6 0.8 copy.16.r_f
  1.4 0.8 copy.17.g_f
  2.1 0.8 copy.18.r_b
  2.9 0.8 copy.19.g_b
  3.7 0.0 copy-start
  3.7 1.6 copy-done
  5.2 0.0 copy-start.1
  5.2 1.2 copy-done.1
  6.5 0.0 copy-start.2
  6.5 1.0 copy-done.2
  7.4 0.0 copy-start.3
  7.4 0.9 copy-done.3
  8.3 0.0 copy-start.4
  8.3 0.9 copy-done.4
  9.2 0.0 copy-start.5
  9.2 1.1 copy-done.5
  10.4 0.0 copy-start.6
  10.4 1.1 copy-done.6
  11.4 0.0 copy-start.7
  11.4 1.0 copy-done.7
  12.4 0.0 copy-start.8
  12.4 0.9 copy-done.8
  13.3 0.0 copy-start.9
  13.3 0.9 copy-done.9
  14.2 162.6 %shard_map.149 = (bf16[16,4096]{1,0:T(8,128)(2,1)S(1)}, bf16[16,4096]{1,0:T(8,128)(2,1)S(1)}) custom-call(bf16[16,4096]{1,0:T(8,128)(2,1)S(1)} %bitcast.16, s32[16,2]{1,0:T(8,128)S(1)} %copy.16.r_f, f32[16,2]{1,0:T(8,128)S(1)} %copy.17.g_f, bf16[16,4096]{1,0:T(8,128)(2,1)S(1)} %bitcast.17, s32[16,2]{1,0:T(8,128)S(1)} %copy.18.r_b, f32[16,2]{1,0:T(8,128)S(1)} %copy.19.g_b, ...), custom_call_target="tpu_custom_call" | custom-call | flops 4000000000 | bytes 8000000 | tf_op jit(solution)/shard_map/pallas_call | solution.py:427
  176.8 0.7 copy.22
  177.4 0.7 copy.23
Async XLA Ops:
  3.7 1.6 copy-start
  5.2 1.2 copy-start.1
  6.5 1.0 copy-start.2
  7.4 0.9 copy-start.3
  8.3 0.9 copy-start.4
  9.2 1.1 copy-start.5
  10.4 1.1 copy-start.6
  11.4 1.0 copy-start.7
  12.4 0.9 copy-start.8
  13.3 0.9 copy-start.9

commit v2 on v1

v2 whole, which is shorter than its diff:
```python
import jax
import jax.numpy as jnp
from jax import lax
from jax.experimental import pallas as pl
from jax.experimental.pallas import tpu as pltpu
from jax.sharding import PartitionSpec as P

GROUP = 8
BASE = 4
OVER = 5
ZN = 16
XN = 4
LINE = 4
NORM = ZN * BASE
LATE = ZN * OVER
CHUNK = NORM + LATE
PIECES = (0, 1, 2)
F, B = 0, 1
MESH = pl.DeviceIdType.MESH


def one_hot(target, width):
    col = lax.broadcasted_iota(jnp.int32, (target.shape[0], width), 1)
    return jnp.where(col == target, 1.0, 0.0).astype(jnp.bfloat16)


def fifth(v):
    return (v * 205) >> 10


def rows_of(count):
    return lax.broadcasted_iota(jnp.int32, (count, 1), 0)


def norm_out():
    r = rows_of(256)
    return one_hot(((r >> 2) & 15) * 16 + (r >> 6) * 4 + (r & 3), 256)


def norm_back():
    r = rows_of(256)
    return one_hot(((r >> 2) & 3) * 64 + (r >> 4) * 4 + (r & 3), 256)


def over_out(half):
    r = rows_of(80)
    g = fifth(r)
    return one_hot(g * 16 + half * 8 + r - 5 * g, 256)


def over_back(half):
    r = rows_of(256)
    j = r & 7
    want = jnp.where((((r >> 3) & 1) == half) & (j < OVER), (r >> 4) * 5 + j, -1)
    one = one_hot(want, 80)
    return jnp.concatenate([one] * XN, axis=1)


def stash_rows(x):
    r = rows_of(CHUNK)
    k = r - NORM
    is_norm = k < 0
    g = jnp.where(is_norm, r >> 2, fifth(k))
    slot = jnp.where(is_norm, r & 3, 4 + k - 5 * g)
    return one_hot(((g & 7) * 8 + x * 2 + (g >> 3)) * 9 + slot, XN * CHUNK)


def dot(a, b):
    return jnp.dot(a, b, preferred_element_type=jnp.float32)


def dot_t(a, b):
    return lax.dot_general(a, b, (((1,), (1,)), ((), ())), preferred_element_type=jnp.float32)


def sigmoid(v):
    return 1.0 / (1.0 + jnp.exp(-v))


def route_ranks(route):
    name = lax.broadcasted_iota(jnp.int32, (8, 16), 0)
    picks = [route[k : k + 1] for k in range(2)]
    hits = jnp.where(picks[0] == name, 1.0, 0.0) + jnp.where(picks[1] == name, 1.0, 0.0)
    row = lax.broadcasted_iota(jnp.int32, (16, 16), 0)
    col = lax.broadcasted_iota(jnp.int32, (16, 16), 1)
    earlier = jnp.where(row < col, 1.0, 0.0).astype(jnp.bfloat16)
    before = dot(hits.astype(jnp.bfloat16), earlier)
    ranks = [
        jnp.sum(jnp.where(pick == name, before, 0.0), axis=0, keepdims=True).astype(jnp.int32) for pick in picks
    ]
    return ranks, jnp.sum(hits, axis=1, keepdims=True)


def choice_match(route, ranks, rows, half=None):
    row = lax.broadcasted_iota(jnp.int32, (rows, 16), 0)
    is_norm = row < 32
    expert = ((row >> 2) & 3) * 2 + (row >> 4)
    slot = jnp.where(is_norm, row & 3, 4 + (row & 7))
    if half is not None:
        slot = jnp.where(is_norm | (((row >> 3) & 1) == half), slot, 99)
    return [
        (slot == ranks[k]) & ((expert == route[k : k + 1]) | jnp.logical_not(is_norm)) for k in range(2)
    ]


def gate_parts(route, gates, ranks, half):
    match = choice_match(route, ranks, 64, half)
    total = jnp.where(match[0], gates[0:1], 0.0) + jnp.where(match[1], gates[1:2], 0.0)
    total = jnp.concatenate([total, jnp.zeros((64, 16), jnp.float32)], axis=0)
    total = jnp.concatenate([total, jnp.zeros((128, 112), jnp.float32)], axis=1)
    total = jnp.transpose(total)[:16, :64]
    high = total.astype(jnp.bfloat16)
    rest = total - high.astype(jnp.float32)
    middle = rest.astype(jnp.bfloat16)
    low = (rest - middle.astype(jnp.float32)).astype(jnp.bfloat16)
    return jnp.concatenate([high, middle, low], axis=0)


def buffers():
    bf16, f32 = jnp.bfloat16, jnp.float32
    out = {
        "xin": pltpu.VMEM((2, 16, 4096), bf16),
        "r_v": pltpu.VMEM((2, 2, 16), jnp.int32),
        "g_v": pltpu.VMEM((2, 2, 16), f32),
        "wgu": pltpu.VMEM((2, 4, 2, 128, 512), bf16),
        "wd": pltpu.VMEM((4, 2, 128, 512), bf16),
        "wgu_s": pltpu.VMEM((2, 4, 128, 512), bf16),
        "wd_s": pltpu.VMEM((4, 128, 512), bf16),
        "saved": pltpu.VMEM((576, 256), bf16),
        "c_no": pltpu.VMEM((256, 256), bf16),
        "c_oo": pltpu.VMEM((2, 80, 256), bf16),
        "c_nb": pltpu.VMEM((256, 256), bf16),
        "c_ob": pltpu.VMEM((2, 256, XN * LATE), bf16),
        "kept": pltpu.VMEM((2, 2 * NORM, 256), f32),
        "kept_o": pltpu.VMEM((LATE, 256), f32),
        "sv_s": pltpu.VMEM((XN, LATE, 256), bf16),
        "sv_r": pltpu.VMEM((XN, LATE, 256), bf16),
        "zsend": pltpu.VMEM((2, ZN, 16, 768), bf16),
        "zrecv": pltpu.VMEM((2, ZN, 16, 768), bf16),
        "wsend": pltpu.VMEM((2, ZN, 16, 768), bf16),
        "wrecv": pltpu.VMEM((2, ZN, 16, 768), bf16),
        "xsend": pltpu.VMEM((2, XN, CHUNK, 512), bf16),
        "xrecv": pltpu.VMEM((2, XN, CHUNK, 512), bf16),
        "xsib": pltpu.VMEM((2, XN, CHUNK, 512), bf16),
        "oret": pltpu.VMEM((2, XN, CHUNK, 512), bf16),
        "orecv": pltpu.VMEM((2, XN, CHUNK, 512), bf16),
        "comb": pltpu.VMEM((2, 16, 4096), bf16),
    }
    for t in (F, B):
        units = 256 if t == F else 128
        parts = 1 if t == F else 2
        out[f"xr_s{t}"] = pltpu.VMEM((XN, 4, LATE, units), bf16)
        out[f"xr_r{t}"] = pltpu.VMEM((XN, 4, LATE, units), bf16)
        for kind, count, rows in (("n", 2, 2 * NORM), ("o", 1, LATE)):
            out[f"own{t}{kind}"] = pltpu.VMEM((count, 4, rows, units), f32)
            out[f"tot{t}{kind}"] = pltpu.VMEM((count, rows, units), f32)
            for name, dests in (("ra", 3), ("rb", 2), ("rc", 1)):
                for way in "sr":
                    out[f"{name}_{way}{t}{kind}"] = pltpu.VMEM((count, dests, rows, units), bf16)
        out[f"hid{t}n"] = pltpu.VMEM((2, 2, parts, 2 * NORM, 512), bf16)
        out[f"hid{t}o"] = pltpu.VMEM((XN, 2, parts, LATE, 512), bf16)
    dma = pltpu.SemaphoreType.DMA
    out["load_sem"] = dma((9,))
    out["wx_sem"] = dma((2, 2))
    for name in ("z", "w"):
        out[name + "_sem"] = dma((2, 2, ZN))
    for name in ("x", "c", "xr", "xg", "xa", "on", "oo"):
        out[name + "_sem"] = dma((2, 2, XN))
    out["sv_sem"] = dma((2, XN))
    for name in ("ra", "rb", "rc", "as"):
        out[name + "_sem"] = dma((2, 2, 3))
    out["ag_ss"] = dma((2, 3, 5))
    out["ag_rs"] = dma((2, 3, LINE))
    out["y_sem"] = dma((2, 2))
    return out


def kernel(x_f, r_f, g_f, x_b, r_b, g_b, wgu_h, wd_h, saved_h, out_f, out_b, *scratch):
    s = dict(zip(buffers(), scratch))
    xin, r_v, g_v = s["xin"], s["r_v"], s["g_v"]
    wgu, wd, wgu_s, wd_s = s["wgu"], s["wd"], s["wgu_s"], s["wd_s"]
    zsend, zrecv, wsend, wrecv = s["zsend"], s["zrecv"], s["wsend"], s["wrecv"]
    xsend, xrecv, xsib, oret, orecv = s["xsend"], s["xrecv"], s["xsib"], s["oret"], s["orecv"]
    comb, kept, kept_o = s["comb"], s["kept"], s["kept_o"]

    pipe = lax.axis_index("pipe")
    expert = lax.axis_index("expert")
    y, h = pipe // 8, pipe % 8
    zl, core = h // 2, h % 2
    x, zh = expert // 2, expert % 2
    g = zh * 8 + h
    side = zl // 2
    is_end = zl % 3 == 0
    is_mid = zl % 3 != 0
    ne, nm, fm, fe = 3 * side, 1 + side, 2 - side, 3 - 3 * side

    def ring_id(gg):
        return (y * 8 + gg % 8, x * 2 + gg // 8)

    def x_id(xx):
        return (pipe, xx * 2 + zh)

    def line_id(zz):
        return (y * 8 + zz * 2 + core, expert)

    def chunk_of(i):
        return (x + XN - i) % XN

    sib_id = (pipe + 1 - 2 * core, expert)
    ends = (((pipe + 8) % 64, expert), ((pipe + 56) % 64, expert))

    def remote(src, dst, ss, rs, dev):
        return pltpu.make_async_remote_copy(
            src_ref=src, dst_ref=dst, send_sem=ss, recv_sem=rs, device_id=dev, device_id_type=MESH
        )

    def pair(name, *at):
        sem = s[name + "_sem"]
        return sem.at[(0,) + at], sem.at[(1,) + at]

    def piece(name, t, q):
        return s[f"{name}{t}n"].at[q] if q < 2 else s[f"{name}{t}o"].at[0]

    def full(t, q):
        return s[f"hid{t}n"].at[q] if q < 2 else s[f"hid{t}o"].at[x]

    def block_at(zz):
        return pl.ds(pl.multiple_of(zz * 128, 128), 128)

    def z_copy(t, d):
        to = (g + d) % ZN
        return remote(zsend.at[t, to], zrecv.at[t, g], *pair("z", t, d), ring_id(to))

    def x_copy(t, d):
        to = (x + d) % XN
        return remote(xsend.at[t, to], xrecv.at[t, x], *pair("x", t, d), x_id(to))

    def c_copy(t, i):
        at = chunk_of(i)
        return remote(xrecv.at[t, at], xsib.at[t, at], *pair("c", t, i), sib_id)

    def sv_copy(i):
        return remote(s["sv_s"].at[i], s["sv_r"].at[i], *pair("sv", i), x_id(chunk_of(i)))

    def xr_copy(t, i):
        return remote(s[f"xr_s{t}"].at[i], s[f"xr_r{t}"].at[i], *pair("xr", t, i), x_id(chunk_of(i)))

    def r_copy(name, t, q):
        to = {"ra": nm, "rb": fm, "rc": ne}[name]
        return remote(piece(name + "_s", t, q), piece(name + "_r", t, q), *pair(name, t, q), line_id(to))

    def ag_copy(t, q, block, to, k):
        here = full(t, q).at[core, :, :, block_at(block)]
        return remote(here, here, s["ag_ss"].at[t, q, k], s["ag_rs"].at[t, q, block], line_id(to))

    def as_copy(t, q):
        here = full(t, q).at[core]
        return remote(here, here, *pair("as", t, q), sib_id)

    def xg_copy(t, i):
        here = s[f"hid{t}o"].at[x, core]
        return remote(here, here, *pair("xg", t, i), x_id((x + i) % XN))

    def xa_copy(t, i):
        here = s[f"hid{t}o"].at[chunk_of(i), core]
        return remote(here, here, *pair("xa", t, i), sib_id)

    def on_copy(t, i):
        rows, to = pl.ds(0, NORM), chunk_of(i)
        return remote(oret.at[t, to, rows], orecv.at[t, x, rows], *pair("on", t, i), x_id(to))

    def oo_copy(t, i):
        rows, to = pl.ds(NORM, LATE), chunk_of(i)
        return remote(oret.at[t, to, rows], orecv.at[t, x, rows], *pair("oo", t, i), x_id(to))

    def w_copy(t, d):
        to = (g + d) % ZN
        return remote(wsend.at[t, to], wrecv.at[t, g], *pair("w", t, d), ring_id(to))

    def y_copy(t):
        return remote(comb.at[t], (out_f, out_b)[t], *pair("y", t), ends[t])

    wx = [
        remote(wgu_h.at[:, :, 1 - core], wgu_s, *pair("wx", 0), sib_id),
        remote(wd_h.at[:, 1 - core], wd_s, *pair("wx", 1), sib_id),
    ]

    moves = (
        (r_b, r_v.at[B]), (x_b, xin.at[B]), (r_f, r_v.at[F]), (x_f, xin.at[F]), (g_f, g_v.at[F]), (g_b, g_v.at[B]),
        (saved_h, s["saved"]), (wgu_h, wgu), (wd_h, wd),
    )
    loads = [pltpu.make_async_copy(a, b, s["load_sem"].at[i]) for i, (a, b) in enumerate(moves)]
    for load in loads:
        load.start()

    barrier = pltpu.get_barrier_semaphore()
    peers = [ring_id((g + d) % ZN) for d in range(1, ZN)]
    peers += [x_id((x + d) % XN) for d in range(1, XN)]
    peers += list(ends)
    for peer in peers:
        pl.semaphore_signal(barrier, inc=1, device_id=peer, device_id_type=MESH)

    for load in loads[:6]:
        load.wait()
    routing = {}
    for t in (B, F):
        route = r_v[t]
        ranks, counts = route_ranks(route)
        match = choice_match(route, ranks, 48)
        pick = jnp.where(match[0] | match[1], 1.0, 0.0).astype(jnp.bfloat16)
        name = lax.broadcasted_iota(jnp.int32, (8, 1), 0)
        mine = jnp.sum(jnp.where(name == expert, counts, 0.0), axis=0, keepdims=True)
        routing[t] = (route, ranks, mine > BASE + 0.5)
        upper = lax.broadcasted_iota(jnp.int32, (16, 256), 0) < 8
        for b in range(8):
            rows = dot(pick, xin[t, :, b * 512 : (b + 1) * 512])
            over = jnp.where(upper, rows[32:48, :256], rows[32:48, 256:]).astype(jnp.bfloat16)
            for hi in range(2):
                zsend[t, hi * 8 + b, :, 0:512] = rows[hi * 16 : hi * 16 + 16].astype(jnp.bfloat16)
                zsend[t, hi * 8 + b, :, 512:768] = over

    def busiest_only(t, value):
        return jnp.where(routing[t][2], value, 0.0)

    pl.semaphore_wait(barrier, len(peers))

    for t in (B, F):
        for d in range(1, ZN):
            z_copy(t, d).start()
        zrecv[t, g] = zsend[t, g]
    for copy in wx:
        copy.start()

    s["c_no"][...] = norm_out()
    s["c_nb"][...] = norm_back()
    for half in range(2):
        s["c_oo"][half] = over_out(half)
        s["c_ob"][half] = over_back(half)
    loads[6].wait()
    for i in range(XN):
        found = dot(stash_rows(chunk_of(i)), s["saved"][...])
        kept[i // 2, (i % 2) * NORM : (i % 2 + 1) * NORM] = found[:NORM]
        late = busiest_only(B, found[NORM:])
        if i == 0:
            kept_o[...] = late
        else:
            s["sv_s"][i] = late.astype(jnp.bfloat16)
            sv_copy(i).start()

    def rows_to_x(t):
        for d in range(1, ZN):
            z_copy(t, d).wait_recv()
        got = zrecv[t].reshape(256, 768)
        norm = dot(s["c_no"][...], got[:, :512]).astype(jnp.bfloat16)
        over = jnp.concatenate(
            [dot(s["c_oo"][0], got[:, 512:]), dot(s["c_oo"][1], got[:, 512:])], axis=1
        ).astype(jnp.bfloat16)
        for xx in range(XN):
            xsend[t, xx, 0:NORM] = norm[xx * NORM : (xx + 1) * NORM]
            xsend[t, xx, NORM:CHUNK] = over
        for d in range(1, XN):
            x_copy(t, d).start()
        xrecv[t, x] = xsend[t, x]
        c_copy(t, 0).start()

    def rows_to_sibling(t):
        for i in range(1, XN):
            x_copy(t, i).wait_recv()
            c_copy(t, i).start()

    def weights(t, dest):
        if t == F:
            return (
                jnp.concatenate([wgu[0, dest, core], wgu[1, dest, core]], axis=0),
                jnp.concatenate([wgu_s[0, dest], wgu_s[1, dest]], axis=0),
            )
        return wd[dest, core], wd_s[dest]

    def late_products(t):
        for i in (1, 2, 3, 0):
            c_copy(t, i).wait_recv()
            at = chunk_of(i)
            for k, dest in enumerate((fe, fm, nm, ne)):
                w_mine, w_other = weights(t, dest)
                part = dot_t(xrecv[t, at, NORM:], w_mine) + dot_t(xsib[t, at, NORM:], w_other)
                part = busiest_only(t, part)
                if i == 0:
                    s[f"own{t}o"][0, k] = part
                else:
                    s[f"xr_s{t}"][i, k] = part.astype(jnp.bfloat16)
            if i > 0:
                xr_copy(t, i).start()

    def norm_products(t):
        for q in range(2):
            ats = [chunk_of(2 * q), chunk_of(2 * q + 1)]
            mine = jnp.concatenate([xrecv[t, at, :NORM] for at in ats], axis=0)
            other = jnp.concatenate([xsib[t, at, :NORM] for at in ats], axis=0)
            for k, dest in enumerate((fe, fm, nm, ne)):
                w_mine, w_other = weights(t, dest)
                part = dot_t(mine, w_mine) + dot_t(other, w_other)
                s[f"own{t}n"][q, k] = part
                if k < 3:
                    s[f"ra_s{t}n"][q, k] = part.astype(jnp.bfloat16)
            ends_send(t, q)

    def ends_send(t, q):
        @pl.when(is_end)
        def _():
            r_copy("ra", t, q).start()

    def late_sum(t):
        for k in range(4):
            total = s[f"own{t}o"][0, k]
            for i in range(1, XN):
                if k == 0:
                    xr_copy(t, i).wait_recv()
                total = total + s[f"xr_r{t}"][i, k].astype(jnp.float32)
            s[f"own{t}o"][0, k] = total
            if k < 3:
                s[f"ra_s{t}o"][0, k] = total.astype(jnp.bfloat16)
        ends_send(t, 2)

    def middles_send(t, q):
        @pl.when(is_mid)
        def _():
            r_copy("ra", t, q).wait_recv()
            own, came = piece("own", t, q), piece("ra_r", t, q)
            for k in range(2):
                piece("rb_s", t, q)[k] = (own[k] + came[k].astype(jnp.float32)).astype(jnp.bfloat16)
            r_copy("rb", t, q).start()

    def middles_return(t, q):
        @pl.when(is_mid)
        def _():
            r_copy("rb", t, q).wait_recv()
            own, came = piece("own", t, q), piece("rb_r", t, q)
            piece("rc_s", t, q)[0] = (own[3] + came[0].astype(jnp.float32)).astype(jnp.bfloat16)
            r_copy("rc", t, q).start()
            near = piece("ra_r", t, q)
            piece("tot", t, q)[...] = own[2] + near[2].astype(jnp.float32) + came[1].astype(jnp.float32)

    def activate(t, q):
        @pl.when(is_end)
        def _():
            r_copy("rc", t, q).wait_recv()
            piece("tot", t, q)[...] = piece("own", t, q)[3] + piece("rc_r", t, q)[0].astype(jnp.float32)

        total = piece("tot", t, q)[...]
        hid = full(t, q)
        if t == F:
            gate, up = total[:, :128], total[:, 128:]
            hid[core, 0, :, block_at(zl)] = (gate * sigmoid(gate) * up).astype(jnp.bfloat16)
        else:
            stash = kept[q] if q < 2 else kept_o[...]
            gate, up = stash[:, :128], stash[:, 128:]
            sig = sigmoid(gate)
            slope = sig * (1.0 + gate * (1.0 - sig))
            hid[core, 0, :, block_at(zl)] = (total * up * slope).astype(jnp.bfloat16)
            hid[core, 1, :, block_at(zl)] = (total * (gate * sig)).astype(jnp.bfloat16)

        @pl.when(is_end)
        def _():
            ag_copy(t, q, ne, nm, 0).start()

        @pl.when(is_mid)
        def _():
            ag_copy(t, q, nm, fm, 1).start()
            ag_copy(t, q, nm, ne, 0).start()

    def relay_near(t, q):
        @pl.when(is_mid)
        def _():
            ag_copy(t, q, ne, nm, 0).wait_recv()
            ag_copy(t, q, ne, fm, 2).start()
            ag_copy(t, q, fm, nm, 0).wait_recv()
            ag_copy(t, q, fm, ne, 3).start()

    def relay_far(t, q):
        @pl.when(is_mid)
        def _():
            ag_copy(t, q, fe, nm, 0).wait_recv()
            ag_copy(t, q, fe, ne, 4).start()

    def units_to_sibling(t, q):
        @pl.when(is_end)
        def _():
            for block in (nm, fm, fe):
                ag_copy(t, q, block, ne, 0).wait_recv()

        as_copy(t, q).start()
        if q == 2:
            for i in range(1, XN):
                xg_copy(t, i).start()

    def down(t, hid):
        if t == F:
            return dot(hid[0, 0], wd[:, 0].reshape(512, 512)) + dot(hid[1, 0], wd[:, 1].reshape(512, 512))
        total = None
        for c in range(2):
            for a in range(2):
                part = dot(hid[c, a], wgu[a, :, c].reshape(512, 512))
                total = part if total is None else total + part
        return total

    def norm_back_to_x(t):
        for q in (1, 0):
            as_copy(t, q).wait_recv()
            made = down(t, s[f"hid{t}n"].at[q]).astype(jnp.bfloat16)
            for i in (2 * q + 1, 2 * q):
                rows = made[(i % 2) * NORM : (i % 2 + 1) * NORM]
                if i == 0:
                    orecv[t, x, 0:NORM] = rows
                else:
                    oret[t, chunk_of(i), 0:NORM] = rows
                    on_copy(t, i).start()

    def late_to_sibling(t):
        for i in range(1, XN):
            xg_copy(t, i).wait_recv()
            xa_copy(t, i).start()

    def late_back_to_x(t):
        for i in (1, 2, 3, 0):
            if i == 0:
                as_copy(t, 2).wait_recv()
            else:
                xa_copy(t, i).wait_recv()
            made = down(t, s[f"hid{t}o"].at[chunk_of(i)])
            made = busiest_only(t, made).astype(jnp.bfloat16)
            if i == 0:
                orecv[t, x, NORM:CHUNK] = made
            else:
                oret[t, chunk_of(i), NORM:CHUNK] = made
                oo_copy(t, i).start()

    def rows_to_sources(t):
        for i in range(1, XN):
            on_copy(t, i).wait_recv()
            oo_copy(t, i).wait_recv()
        norm = orecv[t, :, 0:NORM, :].reshape(XN * NORM, 512)
        wsend[t, :, :, 0:512] = dot(s["c_nb"][...], norm).astype(jnp.bfloat16).reshape(ZN, 16, 512)
        late = orecv[t, :, NORM:CHUNK, :].reshape(XN * LATE, 512)
        over = dot(s["c_ob"][0], late[:, :256]) + dot(s["c_ob"][1], late[:, 256:])
        wsend[t, :, :, 512:768] = over.astype(jnp.bfloat16).reshape(ZN, 16, 256)
        for d in range(1, ZN):
            w_copy(t, d).start()
        wrecv[t, g] = wsend[t, g]

    def combine(t):
        route, ranks, _ = routing[t]
        parts = [gate_parts(route, g_v[t], ranks, half) for half in range(2)]
        for d in range(1, ZN):
            w_copy(t, d).wait_recv()
        for b in range(8):
            for half in range(2):
                lo = half * 256
                rows = jnp.concatenate(
                    [
                        wrecv[t, b, :, lo : lo + 256],
                        wrecv[t, 8 + b, :, lo : lo + 256],
                        wrecv[t, b, :, 512:768],
                        wrecv[t, 8 + b, :, 512:768],
                    ],
                    axis=0,
                )
                mixed = dot(parts[half], rows)
                mixed = mixed[0:16] + mixed[16:32] + mixed[32:48]
                comb[t, :, b * 512 + lo : b * 512 + lo + 256] = mixed.astype(jnp.bfloat16)
        y_copy(t).start()

    rows_to_x(B)
    for load in loads[7:]:
        load.wait()
    for copy in wx:
        copy.wait_recv()
    rows_to_sibling(B)
    late_products(B)
    norm_products(B)
    rows_to_x(F)
    for i in range(1, XN):
        sv_copy(i).wait_recv()
        kept_o[...] += s["sv_r"][i].astype(jnp.float32)
    for q in range(2):
        middles_send(B, q)
    late_sum(B)
    rows_to_sibling(F)
    for q in range(2):
        middles_return(B, q)
    late_products(F)
    for q in range(2):
        activate(B, q)
    middles_send(B, 2)
    norm_products(F)
    for q in range(2):
        relay_near(B, q)
    middles_return(B, 2)
    for q in range(2):
        middles_send(F, q)
    for q in range(2):
        relay_far(B, q)
    activate(B, 2)
    late_sum(F)
    for q in range(2):
        units_to_sibling(B, q)
    for q in range(2):
        middles_return(F, q)
    relay_near(B, 2)
    norm_back_to_x(B)
    for q in range(2):
        activate(F, q)
    relay_far(B, 2)
    middles_send(F, 2)
    units_to_sibling(B, 2)
    for q in range(2):
        relay_near(F, q)
    middles_return(F, 2)
    late_to_sibling(B)
    for q in range(2):
        relay_far(F, q)
    activate(F, 2)
    late_back_to_x(B)
    for q in range(2):
        units_to_sibling(F, q)
    relay_near(F, 2)
    norm_back_to_x(F)
    relay_far(F, 2)
    rows_to_sources(B)
    units_to_sibling(F, 2)
    late_to_sibling(F)
    late_back_to_x(F)
    rows_to_sources(F)
    combine(B)
    combine(F)

    for copy in wx:
        copy.wait_send()
    for i in range(1, XN):
        sv_copy(i).wait_send()
    for t in (B, F):
        for d in range(1, ZN):
            z_copy(t, d).wait_send()
            w_copy(t, d).wait_send()
        for i in range(XN):
            c_copy(t, i).wait_send()
        for i in range(1, XN):
            for copy in (x_copy, xr_copy, xg_copy, xa_copy, on_copy, oo_copy):
                copy(t, i).wait_send()
        for q in PIECES:
            as_copy(t, q).wait_send()

        @pl.when(is_end)
        def _():
            for q in PIECES:
                r_copy("ra", t, q).wait_send()
                ag_copy(t, q, ne, nm, 0).wait_send()

        @pl.when(is_mid)
        def _():
            for q in PIECES:
                r_copy("rb", t, q).wait_send()
                r_copy("rc", t, q).wait_send()
                for k in range(5):
                    ag_copy(t, q, ne, ne, k).wait_send()

    for t in (B, F):
        y_copy(t).wait()


def on_device(x_f, r_f, g_f, x_b, r_b, g_b, gate_up, down, saved):
    in_hbm = pl.BlockSpec(memory_space=pltpu.HBM)
    out = jax.ShapeDtypeStruct((16, 4096), jnp.bfloat16)
    call = pl.pallas_call(
        kernel,
        out_shape=[out, out],
        in_specs=[in_hbm] * 9,
        out_specs=[in_hbm, in_hbm],
        scratch_shapes=list(buffers().values()),
        compiler_params=pltpu.CompilerParams(
            collective_id=0, has_side_effects=True, vmem_limit_bytes=60 * 1024 * 1024
        ),
        cost_estimate=pl.CostEstimate(flops=4 * 10**9, bytes_accessed=8 * 10**6, transcendentals=10**6),
    )
    next_input, prior_gradient = call(
        x_f[0], r_f[0].T, g_f[0].T, x_b[0], r_b[0].T, g_b[0].T,
        gate_up.reshape(2, 4, 2, 128, 512), down.reshape(4, 2, 128, 512), saved[0, 0],
    )
    return next_input[None], prior_gradient[None]


def solution(mesh):
    row = P("pipe", "expert", None)
    wide = P("pipe", "expert", None, None)
    return jax.shard_map(
        on_device,
        mesh=mesh,
        in_specs=(row,) * 6 + (wide,) * 3,
        out_specs=(row, row),
        check_vma=False,
    )
```

time: 179 us -> 133 us (0.74)
  Pallas kernels: 163 us -> 129 us
  local copies, waits for them, and re-layouts: 14.9 us -> 3.14 us
    pallas_call x1, Pallas kernels: 163 us -> 129 us  [on_device(): call(x_f[0], r_f[0].T, g_f[0].T, x_b[0], r_b[0].T, g_b[0].T, gate_up.resh...]
    unnamed x22 -> x2, local copies, waits for them, and re-layouts: 11.9 us -> 3.14 us
    squeeze x4 -> x0, local copies, waits for them, and re-layouts: 3.02 us -> none  [the longest x1 0.76 us: on_device(): r_f[0]]
where the time goes in v2:
time: 133 us
  Pallas kernels  129 us (97%)
  local copies, waits for them, and re-layouts  3.14 us (2%)
    pallas_call x1, Pallas kernels, on_device(): call(x_f[0], r_f[0].T, g_f[0].T, x_b[0], r_b[0].T, g_b[0].T, gate_up.resh...  129 us
    unnamed x2, local copies, waits for them, and re-layouts  3.14 us

profile of v2, /device:TPU:1, one launch (start us, length us, event | category | flops | bytes accessed | tf_op | source)
XLA Modules:
  0.0 133.1 jit_solution(9798871639228817803)
XLA Ops:
  0.6 129.3 %shard_map.104 = (bf16[16,4096]{1,0:T(8,128)(2,1)}, bf16[16,4096]{1,0:T(8,128)(2,1)}) custom-call(bf16[16,4096]{1,0:T(8,128)(2,1)} %bitcast.24, s32[2,16]{1,0:T(2,128)} %bitcast.26, f32[2,16]{1,0:T(2,128)} %bitcast.27, bf16[16,4096]{1,0:T(8,128)(2,1)} %bitcast.25, s32[2,16]{1,0:T(2,128)} %bitcast.28, f32[2,16]{1,0:T(2,128)} %bitcast.29, ...), custom_call_target="tpu_custom_call" | custom-call | flops 4000000000 | bytes 8000000 | tf_op jit(solution)/shard_map/pallas_call | solution.py:684
  130.0 1.6 %copy.13 = bf16[1,16,4096]{2,1,0:T(8,128)(2,1)} copy(bf16[1,16,4096]{2,1,0:T(8,128)(2,1)} %bitcast.20) | data formatting | bytes 262144
  131.6 1.6 %copy.14 = bf16[1,16,4096]{2,1,0:T(8,128)(2,1)} copy(bf16[1,16,4096]{2,1,0:T(8,128)(2,1)} %bitcast.19) | data formatting | bytes 262144

commit v3 on v2

v3 whole, which is shorter than its diff:
```python
import jax
import jax.numpy as jnp
from jax import lax
from jax.experimental import pallas as pl
from jax.experimental.pallas import tpu as pltpu
from jax.sharding import PartitionSpec as P

GROUP = 8
BASE = 4
OVER = 5
ZN = 16
XN = 4
LINE = 4
NORM = ZN * BASE
LATE = ZN * OVER
CHUNK = NORM + LATE
F, B = 0, 1
KINDS = {"n": NORM, "o": LATE}
WIDTH = {"n": 512, "o": 256}
STREAMS = ((B, "o"), (B, "n"), (F, "o"), (F, "n"))
Z_ORDER = (8, 7, 9, 6, 10, 5, 11, 4, 12, 3, 13, 2, 14, 1, 15)
LAG = (0, 1, 2, 3)
SHIFTS = (2, 1, 3, 0)
PIECES = {"n": 2, "o": 1}
MESH = pl.DeviceIdType.MESH


def one_hot(target, width):
    col = lax.broadcasted_iota(jnp.int32, (target.shape[0], width), 1)
    return jnp.where(col == target, 1.0, 0.0).astype(jnp.bfloat16)


def fifth(v):
    return (v * 205) >> 10


def rows_of(count):
    return lax.broadcasted_iota(jnp.int32, (count, 1), 0)


def norm_out():
    r = rows_of(256)
    return one_hot(((r >> 2) & 15) * 16 + (r >> 6) * 4 + (r & 3), 256)


def norm_back():
    r = rows_of(256)
    return one_hot(((r >> 2) & 3) * 64 + (r >> 4) * 4 + (r & 3), 256)


def over_out(half):
    r = rows_of(80)
    g = fifth(r)
    return one_hot(g * 16 + half * 8 + r - 5 * g, 256)


def over_back(half):
    r = rows_of(256)
    j = r & 7
    want = jnp.where((((r >> 3) & 1) == half) & (j < OVER), (r >> 4) * 5 + j, -1)
    one = one_hot(want, 80)
    return jnp.concatenate([one] * XN, axis=1)


def stash_rows(x):
    r = rows_of(CHUNK)
    k = r - NORM
    is_norm = k < 0
    g = jnp.where(is_norm, r >> 2, fifth(k))
    slot = jnp.where(is_norm, r & 3, 4 + k - 5 * g)
    return one_hot(((g & 7) * 8 + x * 2 + (g >> 3)) * 9 + slot, XN * CHUNK)


def dot(a, b):
    return jnp.dot(a, b, preferred_element_type=jnp.float32)


def dot_t(a, b):
    return lax.dot_general(a, b, (((1,), (1,)), ((), ())), preferred_element_type=jnp.float32)


def sigmoid(v):
    return 1.0 / (1.0 + jnp.exp(-v))


def route_ranks(route):
    name = lax.broadcasted_iota(jnp.int32, (8, 16), 0)
    picks = [route[k : k + 1] for k in range(2)]
    hits = jnp.where(picks[0] == name, 1.0, 0.0) + jnp.where(picks[1] == name, 1.0, 0.0)
    row = lax.broadcasted_iota(jnp.int32, (16, 16), 0)
    col = lax.broadcasted_iota(jnp.int32, (16, 16), 1)
    earlier = jnp.where(row < col, 1.0, 0.0).astype(jnp.bfloat16)
    before = dot(hits.astype(jnp.bfloat16), earlier)
    ranks = [
        jnp.sum(jnp.where(pick == name, before, 0.0), axis=0, keepdims=True).astype(jnp.int32) for pick in picks
    ]
    return ranks, jnp.sum(hits, axis=1, keepdims=True)


def choice_match(route, ranks, rows, half=None):
    row = lax.broadcasted_iota(jnp.int32, (rows, 16), 0)
    is_norm = row < 32
    expert = ((row >> 2) & 3) * 2 + (row >> 4)
    slot = jnp.where(is_norm, row & 3, 4 + (row & 7))
    if half is not None:
        slot = jnp.where(is_norm | (((row >> 3) & 1) == half), slot, 99)
    return [
        (slot == ranks[k]) & ((expert == route[k : k + 1]) | jnp.logical_not(is_norm)) for k in range(2)
    ]


def gate_parts(route, gates, ranks, half):
    match = choice_match(route, ranks, 64, half)
    total = jnp.where(match[0], gates[0:1], 0.0) + jnp.where(match[1], gates[1:2], 0.0)
    total = jnp.concatenate([total, jnp.zeros((64, 16), jnp.float32)], axis=0)
    total = jnp.concatenate([total, jnp.zeros((128, 112), jnp.float32)], axis=1)
    total = jnp.transpose(total)[:16, :64]
    high = total.astype(jnp.bfloat16)
    rest = total - high.astype(jnp.float32)
    middle = rest.astype(jnp.bfloat16)
    low = (rest - middle.astype(jnp.float32)).astype(jnp.bfloat16)
    return jnp.concatenate([high, middle, low], axis=0)


def buffers():
    bf16, f32 = jnp.bfloat16, jnp.float32
    out = {
        "xin": pltpu.VMEM((2, 16, 4096), bf16),
        "r_v": pltpu.VMEM((2, 2, 16), jnp.int32),
        "g_v": pltpu.VMEM((2, 2, 16), f32),
        "wgu": pltpu.VMEM((2, 4, 2, 128, 512), bf16),
        "wd": pltpu.VMEM((4, 2, 128, 512), bf16),
        "wgu_s": pltpu.VMEM((2, 4, 128, 512), bf16),
        "wd_s": pltpu.VMEM((4, 128, 512), bf16),
        "up_f": pltpu.VMEM((2, 512, 4 * 256), bf16),
        "up_b": pltpu.VMEM((2, 512, 4 * 128), bf16),
        "saved": pltpu.VMEM((576, 256), bf16),
        "c_no": pltpu.VMEM((256, 256), bf16),
        "c_oo": pltpu.VMEM((2, 80, 256), bf16),
        "c_nb": pltpu.VMEM((256, 256), bf16),
        "c_ob": pltpu.VMEM((2, 256, XN * LATE), bf16),
        "kept_n": pltpu.VMEM((2, 2 * NORM, 256), f32),
        "kept_o": pltpu.VMEM((1, LATE, 256), f32),
        "sv_s": pltpu.VMEM((XN, LATE, 256), bf16),
        "sv_r": pltpu.VMEM((XN, LATE, 256), bf16),
        "mix": pltpu.VMEM((2, 16, 4096), f32),
        "comb": pltpu.VMEM((2, 16, 4096), bf16),
    }
    for kind, rows in KINDS.items():
        for name in ("zsend", "zrecv", "wsend", "wrecv"):
            out[name + kind] = pltpu.VMEM((2, ZN, 16, WIDTH[kind]), bf16)
        for name in ("xsend", "xrecv", "xsib", "oret", "orecv"):
            out[name + kind] = pltpu.VMEM((2, XN, rows, 512), bf16)
    for t in (F, B):
        units = 256 if t == F else 128
        parts = 1 if t == F else 2
        out[f"xr_own{t}"] = pltpu.VMEM((4, LATE, units), f32)
        out[f"xr_s{t}"] = pltpu.VMEM((XN, 4, LATE, units), bf16)
        out[f"xr_r{t}"] = pltpu.VMEM((XN, 4, LATE, units), bf16)
        for kind, rows in (("n", 2 * NORM), ("o", LATE)):
            out[f"own{t}{kind}"] = pltpu.VMEM((PIECES[kind], rows, units), f32)
            for way in "sr":
                out[f"rs_{way}{t}{kind}"] = pltpu.VMEM((PIECES[kind], 3, rows, units), bf16)
            count = 2 if kind == "n" else XN
            out[f"hid{t}{kind}"] = pltpu.VMEM((count, 2, parts, rows, 512), bf16)
    dma = pltpu.SemaphoreType.DMA
    out["load_sem"] = dma((9,))
    out["wx_sem"] = dma((2, 2))
    for kind in KINDS:
        for name in ("z", "w"):
            out[name + kind + "_sem"] = dma((2, 2, ZN))
        for name in ("x", "c", "b"):
            out[name + kind + "_sem"] = dma((2, 2, XN))
        out["as" + kind + "_sem"] = dma((2, 2, PIECES[kind]))
        for name in ("rs", "ag"):
            out[name + kind + "_sem"] = dma((2, 2, PIECES[kind], 3))
    for name in ("xr", "xg", "xa"):
        out[name + "_sem"] = dma((2, 2, XN))
    out["sv_sem"] = dma((2, XN))
    out["y_sem"] = dma((2, 2))
    return out


def kernel(x_f, r_f, g_f, x_b, r_b, g_b, wgu_h, wd_h, saved_h, out_f, out_b, *scratch):
    s = dict(zip(buffers(), scratch))
    xin, r_v, g_v = s["xin"], s["r_v"], s["g_v"]
    wgu, wd, wgu_s, wd_s = s["wgu"], s["wd"], s["wgu_s"], s["wd_s"]
    comb, mix = s["comb"], s["mix"]

    pipe = lax.axis_index("pipe")
    expert = lax.axis_index("expert")
    y, h = pipe // 8, pipe % 8
    zl, core = h // 2, h % 2
    x, zh = expert // 2, expert % 2
    g = zh * 8 + h
    def ring_id(gg):
        return (y * 8 + gg % 8, x * 2 + gg // 8)

    def x_id(xx):
        return (pipe, xx * 2 + zh)

    def line_id(zz):
        return (y * 8 + zz * 2 + core, expert)

    def chunk_of(i):
        return (x + XN - i) % XN

    sib_id = (pipe + 1 - 2 * core, expert)
    ends = (((pipe + 8) % 64, expert), ((pipe + 56) % 64, expert))

    def remote(src, dst, ss, rs, dev):
        return pltpu.make_async_remote_copy(
            src_ref=src, dst_ref=dst, send_sem=ss, recv_sem=rs, device_id=dev, device_id_type=MESH
        )

    def pair(name, *at):
        sem = s[name + "_sem"]
        return sem.at[(0,) + at], sem.at[(1,) + at]

    def piece(name, st, q):
        return s[f"{name}{st[0]}{st[1]}"].at[q]

    def block_at(zz):
        return pl.ds(pl.multiple_of(zz * 128, 128), 128)

    def z_copy(st, d):
        t, kind = st
        to = (g + d) % ZN
        return remote(s["zsend" + kind].at[t, to], s["zrecv" + kind].at[t, g], *pair("z" + kind, t, d), ring_id(to))

    def x_copy(st, d):
        t, kind = st
        to = (x + d) % XN
        return remote(s["xsend" + kind].at[t, to], s["xrecv" + kind].at[t, x], *pair("x" + kind, t, d), x_id(to))

    def c_copy(st, i):
        t, kind = st
        at = chunk_of(i)
        return remote(s["xrecv" + kind].at[t, at], s["xsib" + kind].at[t, at], *pair("c" + kind, t, i), sib_id)

    def units_of(st, q):
        return piece("hid", st, q if st[1] == "n" else x)

    def sv_copy(i):
        return remote(s["sv_s"].at[i], s["sv_r"].at[i], *pair("sv", i), x_id(chunk_of(i)))

    def xr_copy(t, i):
        return remote(s[f"xr_s{t}"].at[i], s[f"xr_r{t}"].at[i], *pair("xr", t, i), x_id(chunk_of(i)))

    def rs_copy(st, q, k):
        src, dst = piece("rs_s", st, q).at[k], piece("rs_r", st, q).at[k]
        return remote(src, dst, *pair("rs" + st[1], st[0], q, k), line_id((zl + SHIFTS[k]) % LINE))

    def ag_copy(st, q, k):
        here = units_of(st, q).at[core, :, :, block_at(zl)]
        return remote(here, here, *pair("ag" + st[1], st[0], q, k), line_id((zl + SHIFTS[k]) % LINE))

    def as_copy(st, q):
        here = units_of(st, q).at[core]
        return remote(here, here, *pair("as" + st[1], st[0], q), sib_id)

    def xg_copy(t, i):
        here = s[f"hid{t}o"].at[x, core]
        return remote(here, here, *pair("xg", t, i), x_id((x + i) % XN))

    def xa_copy(t, i):
        here = s[f"hid{t}o"].at[chunk_of(i), core]
        return remote(here, here, *pair("xa", t, i), sib_id)

    def b_copy(st, i):
        t, kind = st
        to = chunk_of(i)
        return remote(s["oret" + kind].at[t, to], s["orecv" + kind].at[t, x], *pair("b" + kind, t, i), x_id(to))

    def w_copy(st, d):
        t, kind = st
        to = (g + d) % ZN
        return remote(s["wsend" + kind].at[t, to], s["wrecv" + kind].at[t, g], *pair("w" + kind, t, d), ring_id(to))

    def y_copy(t):
        return remote(comb.at[t], (out_f, out_b)[t], *pair("y", t), ends[t])

    wx = [
        remote(wgu_h.at[:, :, 1 - core], wgu_s, *pair("wx", 0), sib_id),
        remote(wd_h.at[:, 1 - core], wd_s, *pair("wx", 1), sib_id),
    ]

    moves = (
        (r_b, r_v.at[B]), (x_b, xin.at[B]), (r_f, r_v.at[F]), (x_f, xin.at[F]), (g_f, g_v.at[F]), (g_b, g_v.at[B]),
        (saved_h, s["saved"]), (wgu_h, wgu), (wd_h, wd),
    )
    loads = [pltpu.make_async_copy(a, b, s["load_sem"].at[i]) for i, (a, b) in enumerate(moves)]
    for load in loads:
        load.start()

    barrier = pltpu.get_barrier_semaphore()
    peers = [ring_id((g + d) % ZN) for d in range(1, ZN)]
    peers += [x_id((x + d) % XN) for d in range(1, XN)]
    peers += list(ends)
    for peer in peers:
        pl.semaphore_signal(barrier, inc=1, device_id=peer, device_id_type=MESH)

    for load in loads[:6]:
        load.wait()
    routing = {}
    for t in (B, F):
        route = r_v[t]
        ranks, counts = route_ranks(route)
        match = choice_match(route, ranks, 48)
        pick = jnp.where(match[0] | match[1], 1.0, 0.0).astype(jnp.bfloat16)
        name = lax.broadcasted_iota(jnp.int32, (8, 1), 0)
        mine = jnp.sum(jnp.where(name == expert, counts, 0.0), axis=0, keepdims=True)
        routing[t] = (route, ranks, mine > BASE + 0.5)
        upper = lax.broadcasted_iota(jnp.int32, (16, 256), 0) < 8
        for b in range(8):
            rows = dot(pick, xin[t, :, b * 512 : (b + 1) * 512])
            over = jnp.where(upper, rows[32:48, :256], rows[32:48, 256:]).astype(jnp.bfloat16)
            for hi in range(2):
                s["zsendn"][t, hi * 8 + b] = rows[hi * 16 : hi * 16 + 16].astype(jnp.bfloat16)
                s["zsendo"][t, hi * 8 + b] = over

    def busiest_only(t, value):
        return jnp.where(routing[t][2], value, 0.0)

    pl.semaphore_wait(barrier, len(peers))

    def rows_to_ring(st):
        t, kind = st
        for d in Z_ORDER:
            z_copy(st, d).start()
        s["zrecv" + kind][t, g] = s["zsend" + kind][t, g]

    rows_to_ring(STREAMS[0])
    for copy in wx:
        copy.start()
    rows_to_ring(STREAMS[1])

    s["c_no"][...] = norm_out()
    s["c_nb"][...] = norm_back()
    for half in range(2):
        s["c_oo"][half] = over_out(half)
        s["c_ob"][half] = over_back(half)
    loads[6].wait()
    for i in range(XN):
        found = dot(stash_rows(chunk_of(i)), s["saved"][...])
        s["kept_n"][i // 2, (i % 2) * NORM : (i % 2 + 1) * NORM] = found[:NORM]
        late = busiest_only(B, found[NORM:])
        if i == 0:
            s["kept_o"][0] = late
        else:
            s["sv_s"][i] = late.astype(jnp.bfloat16)
            sv_copy(i).start()

    def rows_to_x(st):
        t, kind = st
        for d in range(1, ZN):
            z_copy(st, d).wait_recv()
        got = s["zrecv" + kind][t].reshape(256, WIDTH[kind])
        if kind == "n":
            moved = dot(s["c_no"][...], got).astype(jnp.bfloat16)
        else:
            moved = jnp.concatenate([dot(s["c_oo"][0], got), dot(s["c_oo"][1], got)], axis=1).astype(jnp.bfloat16)
        for xx in range(XN):
            s["xsend" + kind][t, xx] = moved[xx * NORM : (xx + 1) * NORM] if kind == "n" else moved
        for d in (2, 1, 3):
            x_copy(st, d).start()
        s["xrecv" + kind][t, x] = s["xsend" + kind][t, x]
        c_copy(st, 0).start()

    def rows_to_sibling(st):
        for i in (1, 3, 2):
            x_copy(st, i).wait_recv()
            c_copy(st, i).start()

    rows_to_ring(STREAMS[2])
    rows_to_ring(STREAMS[3])

    for load in loads[7:]:
        load.wait()
    for copy in wx:
        copy.wait_recv()
    for k, shift in enumerate(SHIFTS):
        dest = (zl + shift) % LINE
        at = k * 128
        s["up_b"][0, :, at : at + 128] = jnp.transpose(wd[dest, core])
        s["up_b"][1, :, at : at + 128] = jnp.transpose(wd_s[dest])
        for a in range(2):
            at = k * 256 + a * 128
            s["up_f"][0, :, at : at + 128] = jnp.transpose(wgu[a, dest, core])
            s["up_f"][1, :, at : at + 128] = jnp.transpose(wgu_s[a, dest])

    def products(st):
        t, kind = st
        up = s["up_f"] if t == F else s["up_b"]
        units = 256 if t == F else 128
        for i in range(XN):
            c_copy(st, i).wait_recv()
        ats = [chunk_of(i) for i in range(XN)]
        mine = jnp.concatenate([s["xrecv" + kind][t, at] for at in ats], axis=0)
        other = jnp.concatenate([s["xsib" + kind][t, at] for at in ats], axis=0)
        for k in range(4):
            lanes = slice(k * units, (k + 1) * units)
            part = dot(mine, up[0, :, lanes]) + dot(other, up[1, :, lanes])
            if kind == "o":
                part = busiest_only(t, part)
                s[f"xr_own{t}"][k] = part[:LATE]
                for i in range(1, XN):
                    s[f"xr_s{t}"][i, k] = part[i * LATE : (i + 1) * LATE].astype(jnp.bfloat16)
                continue
            for q in range(2):
                rows = part[q * 2 * NORM : (q + 1) * 2 * NORM]
                if k == 3:
                    piece("own", st, q)[...] = rows
                else:
                    piece("rs_s", st, q)[k] = rows.astype(jnp.bfloat16)
                    rs_copy(st, q, k).start()
        if kind == "o":
            for i in (2, 1, 3):
                xr_copy(t, i).start()

    def spread_sum(st):
        t = st[0]
        for i in range(1, XN):
            xr_copy(t, i).wait_recv()
        for k in range(4):
            total = s[f"xr_own{t}"][k]
            for i in range(1, XN):
                total = total + s[f"xr_r{t}"][i, k].astype(jnp.float32)
            if k == 3:
                piece("own", st, 0)[...] = total
            else:
                piece("rs_s", st, 0)[k] = total.astype(jnp.bfloat16)
                rs_copy(st, 0, k).start()

    def activate(st):
        for q in range(PIECES[st[1]]):
            total = piece("own", st, q)[...]
            for k in range(3):
                rs_copy(st, q, k).wait_recv()
                total = total + piece("rs_r", st, q)[k].astype(jnp.float32)
            hid = units_of(st, q)
            if st[0] == F:
                gate, up = total[:, :128], total[:, 128:]
                hid[core, 0, :, block_at(zl)] = (gate * sigmoid(gate) * up).astype(jnp.bfloat16)
            else:
                stash = s["kept_" + st[1]][q]
                gate, up = stash[:, :128], stash[:, 128:]
                sig = sigmoid(gate)
                slope = sig * (1.0 + gate * (1.0 - sig))
                hid[core, 0, :, block_at(zl)] = (total * up * slope).astype(jnp.bfloat16)
                hid[core, 1, :, block_at(zl)] = (total * (gate * sig)).astype(jnp.bfloat16)
            for k in range(3):
                ag_copy(st, q, k).start()

    def units_to_sibling(st):
        for q in range(PIECES[st[1]]):
            for k in range(3):
                ag_copy(st, q, k).wait_recv()
            as_copy(st, q).start()
        if st[1] == "o":
            for i in (2, 1, 3):
                xg_copy(st[0], i).start()

    def spread_units(st):
        for i in (1, 3, 2):
            xg_copy(st[0], i).wait_recv()
            xa_copy(st[0], i).start()

    def down(t, hid):
        def rows(c, a):
            return jnp.concatenate([one[c, a] for one in hid], axis=0)

        if t == F:
            return dot(rows(0, 0), wd[:, 0].reshape(512, 512)) + dot(rows(1, 0), wd[:, 1].reshape(512, 512))
        total = None
        for c in range(2):
            for a in range(2):
                part = dot(rows(c, a), wgu[a, :, c].reshape(512, 512))
                total = part if total is None else total + part
        return total

    def back_to_x(st):
        t, kind = st
        rows = KINDS[kind]
        if kind == "o":
            as_copy(st, 0).wait_recv()
            for i in range(1, XN):
                xa_copy(t, i).wait_recv()
            hid = [s[f"hid{t}o"].at[chunk_of(i)] for i in range(XN)]
            made = busiest_only(t, down(t, hid)).astype(jnp.bfloat16)
            for i in range(XN):
                part = made[i * rows : (i + 1) * rows]
                if i == 0:
                    s["orecvo"][t, x] = part
                else:
                    s["oreto"][t, chunk_of(i)] = part
                    b_copy(st, i).start()
            return
        for q in (1, 0):
            as_copy(st, q).wait_recv()
            made = down(t, [piece("hid", st, q)]).astype(jnp.bfloat16)
            for i in (2 * q, 2 * q + 1):
                part = made[(i % 2) * rows : (i % 2 + 1) * rows]
                if i == 0:
                    s["orecv" + kind][t, x] = part
                else:
                    s["oret" + kind][t, chunk_of(i)] = part
                    b_copy(st, i).start()

    def rows_to_sources(st):
        t, kind = st
        for i in range(1, XN):
            b_copy(st, i).wait_recv()
        got = s["orecv" + kind][t].reshape(XN * KINDS[kind], 512)
        if kind == "n":
            moved = dot(s["c_nb"][...], got)
        else:
            moved = dot(s["c_ob"][0], got[:, :256]) + dot(s["c_ob"][1], got[:, 256:])
        s["wsend" + kind][t] = moved.astype(jnp.bfloat16).reshape(ZN, 16, WIDTH[kind])
        for d in range(1, ZN):
            w_copy(st, d).start()
        s["wrecv" + kind][t, g] = s["wsend" + kind][t, g]

    begun = set()

    def combine(st):
        t, kind = st
        route, ranks, _ = routing[t]
        for d in range(1, ZN):
            w_copy(st, d).wait_recv()
        got = s["wrecv" + kind]
        for half in range(2):
            parts = gate_parts(route, g_v[t], ranks, half)
            parts = parts[:, 0:32] if kind == "n" else parts[:, 32:64]
            for b in range(8):
                rows = jnp.concatenate([got[t, b], got[t, 8 + b]], axis=0)
                if kind == "n":
                    rows = rows[:, half * 256 : (half + 1) * 256]
                mixed = dot(parts, rows)
                mixed = mixed[0:16] + mixed[16:32] + mixed[32:48]
                at = pl.ds(b * 512 + half * 256, 256)
                if t in begun:
                    comb[t, :, at] = (mix[t, :, at] + mixed).astype(jnp.bfloat16)
                else:
                    mix[t, :, at] = mixed
        if t in begun:
            y_copy(t).start()
        begun.add(t)

    def late_stash(st):
        if st[0] == B:
            for i in range(1, XN):
                sv_copy(i).wait_recv()
                s["kept_o"][0] += s["sv_r"][i].astype(jnp.float32)
        spread_sum(st)

    first = [rows_to_x, rows_to_sibling, products]
    last = [back_to_x, rows_to_sources, combine]
    steps = {
        "n": first + [activate, units_to_sibling] + last,
        "o": first + [late_stash, activate, units_to_sibling, spread_units] + last,
    }
    for turn in range(len(steps["o"]) + max(LAG)):
        for st, lag in zip(STREAMS, LAG):
            if 0 <= turn - lag < len(steps[st[1]]):
                steps[st[1]][turn - lag](st)

    for copy in wx:
        copy.wait_send()
    for st in STREAMS:
        for d in range(1, ZN):
            z_copy(st, d).wait_send()
            w_copy(st, d).wait_send()
        for i in range(XN):
            c_copy(st, i).wait_send()
        for i in range(1, XN):
            x_copy(st, i).wait_send()
            b_copy(st, i).wait_send()
        for q in range(PIECES[st[1]]):
            as_copy(st, q).wait_send()
            for k in range(3):
                rs_copy(st, q, k).wait_send()
                ag_copy(st, q, k).wait_send()
    for i in range(1, XN):
        sv_copy(i).wait_send()
        for t in (B, F):
            for copy in (xr_copy, xg_copy, xa_copy):
                copy(t, i).wait_send()
    for t in (B, F):
        y_copy(t).wait()


def on_device(x_f, r_f, g_f, x_b, r_b, g_b, gate_up, down, saved):
    in_hbm = pl.BlockSpec(memory_space=pltpu.HBM)
    out = jax.ShapeDtypeStruct((16, 4096), jnp.bfloat16)
    call = pl.pallas_call(
        kernel,
        out_shape=[out, out],
        in_specs=[in_hbm] * 9,
        out_specs=[in_hbm, in_hbm],
        scratch_shapes=list(buffers().values()),
        compiler_params=pltpu.CompilerParams(
            collective_id=0, has_side_effects=True, vmem_limit_bytes=60 * 1024 * 1024
        ),
        cost_estimate=pl.CostEstimate(flops=4 * 10**9, bytes_accessed=8 * 10**6, transcendentals=10**6),
    )
    next_input, prior_gradient = call(
        x_f[0], r_f[0].T, g_f[0].T, x_b[0], r_b[0].T, g_b[0].T,
        gate_up.reshape(2, 4, 2, 128, 512), down.reshape(4, 2, 128, 512), saved[0, 0],
    )
    return next_input[None], prior_gradient[None]


def solution(mesh):
    row = P("pipe", "expert", None)
    wide = P("pipe", "expert", None, None)
    return jax.shard_map(
        on_device,
        mesh=mesh,
        in_specs=(row,) * 6 + (wide,) * 3,
        out_specs=(row, row),
        check_vma=False,
    )
```

time: 133 us -> 123 us (0.925)
  Pallas kernels: 129 us -> 119 us
    pallas_call x1, Pallas kernels: 129 us -> 119 us  [on_device(): call(x_f[0], r_f[0].T, g_f[0].T, x_b[0], r_b[0].T, g_b[0].T, gate_up.resh...]
where the time goes in v3:
time: 123 us
  Pallas kernels  119 us (97%)
  local copies, waits for them, and re-layouts  3.14 us (3%)
    pallas_call x1, Pallas kernels, on_device(): call(x_f[0], r_f[0].T, g_f[0].T, x_b[0], r_b[0].T, g_b[0].T, gate_up.resh...  119 us
    unnamed x2, local copies, waits for them, and re-layouts  3.14 us

profile of v3, /device:TPU:1, one launch (start us, length us, event | category | flops | bytes accessed | tf_op | source)
XLA Modules:
  0.0 122.6 jit_solution(15218482801643411910)
XLA Ops:
  0.6 118.8 %shard_map.104 = (bf16[16,4096]{1,0:T(8,128)(2,1)}, bf16[16,4096]{1,0:T(8,128)(2,1)}) custom-call(bf16[16,4096]{1,0:T(8,128)(2,1)} %bitcast.24, s32[2,16]{1,0:T(2,128)} %bitcast.26, f32[2,16]{1,0:T(2,128)} %bitcast.27, bf16[16,4096]{1,0:T(8,128)(2,1)} %bitcast.25, s32[2,16]{1,0:T(2,128)} %bitcast.28, f32[2,16]{1,0:T(2,128)} %bitcast.29, ...), custom_call_target="tpu_custom_call" | custom-call | flops 4000000000 | bytes 8000000 | tf_op jit(solution)/shard_map/pallas_call | solution.py:607
  119.5 1.6 %copy.13 = bf16[1,16,4096]{2,1,0:T(8,128)(2,1)} copy(bf16[1,16,4096]{2,1,0:T(8,128)(2,1)} %bitcast.20) | data formatting | bytes 262144
  121.0 1.6 %copy.14 = bf16[1,16,4096]{2,1,0:T(8,128)(2,1)} copy(bf16[1,16,4096]{2,1,0:T(8,128)(2,1)} %bitcast.19) | data formatting | bytes 262144

commit v4 on v3

--- a/solution.py
+++ b/solution.py
@@ -19,8 +19,13 @@
 WIDTH = {"n": 512, "o": 256}
 STREAMS = ((B, "o"), (B, "n"), (F, "o"), (F, "n"))
 Z_ORDER = (8, 7, 9, 6, 10, 5, 11, 4, 12, 3, 13, 2, 14, 1, 15)
-LAG = (0, 1, 2, 3)
-SHIFTS = (2, 1, 3, 0)
+W_ORDER = Z_ORDER + (0,)
+ORDER = (
+    0, 10, 1, 2, 11, 30, 12, 20, 3, 31,
+    13, 32, 4, 21, 22, 14, 33, 23, 5, 15,
+    34, 24, 16, 35, 17, 25, 36, 6, 37, 18,
+    7, 26, 27, 38, 8, 28, 39, 19, 9, 29,
+)
 PIECES = {"n": 2, "o": 1}
 MESH = pl.DeviceIdType.MESH
 
@@ -127,7 +132,8 @@
     out = {
         "xin": pltpu.VMEM((2, 16, 4096), bf16),
         "r_v": pltpu.VMEM((2, 2, 16), jnp.int32),
-        "g_v": pltpu.VMEM((2, 2, 16), f32),
+        "rn_v": pltpu.VMEM((2, 2, 16), jnp.int32),
+        "gn_v": pltpu.VMEM((2, 2, 16), f32),
         "wgu": pltpu.VMEM((2, 4, 2, 128, 512), bf16),
         "wd": pltpu.VMEM((4, 2, 128, 512), bf16),
         "wgu_s": pltpu.VMEM((2, 4, 128, 512), bf16),
@@ -158,13 +164,17 @@
         out[f"xr_s{t}"] = pltpu.VMEM((XN, 4, LATE, units), bf16)
         out[f"xr_r{t}"] = pltpu.VMEM((XN, 4, LATE, units), bf16)
         for kind, rows in (("n", 2 * NORM), ("o", LATE)):
-            out[f"own{t}{kind}"] = pltpu.VMEM((PIECES[kind], rows, units), f32)
+            out[f"own{t}{kind}"] = pltpu.VMEM((PIECES[kind], 2, rows, units), f32)
             for way in "sr":
-                out[f"rs_{way}{t}{kind}"] = pltpu.VMEM((PIECES[kind], 3, rows, units), bf16)
+                if kind == "o":
+                    out[f"rs_{way}{t}o"] = pltpu.VMEM((1, 3, rows, units), bf16)
+                else:
+                    out[f"na_{way}{t}n"] = pltpu.VMEM((2, 2, rows, units), bf16)
+                    out[f"fa_{way}{t}n"] = pltpu.VMEM((2, rows, units), bf16)
             count = 2 if kind == "n" else XN
             out[f"hid{t}{kind}"] = pltpu.VMEM((count, 2, parts, rows, 512), bf16)
     dma = pltpu.SemaphoreType.DMA
-    out["load_sem"] = dma((9,))
+    out["load_sem"] = dma((7,))
     out["wx_sem"] = dma((2, 2))
     for kind in KINDS:
         for name in ("z", "w"):
@@ -176,14 +186,17 @@
             out[name + kind + "_sem"] = dma((2, 2, PIECES[kind], 3))
     for name in ("xr", "xg", "xa"):
         out[name + "_sem"] = dma((2, 2, XN))
+    for name in ("na", "fa"):
+        out[name + "_sem"] = dma((2, 2, 2))
     out["sv_sem"] = dma((2, XN))
-    out["y_sem"] = dma((2, 2))
+    out["y_sem"] = dma((2, 2, 2))
+    out["out_sem"] = dma((2,))
     return out
 
 
 def kernel(x_f, r_f, g_f, x_b, r_b, g_b, wgu_h, wd_h, saved_h, out_f, out_b, *scratch):
     s = dict(zip(buffers(), scratch))
-    xin, r_v, g_v = s["xin"], s["r_v"], s["g_v"]
+    xin, r_v = s["xin"], s["r_v"]
     wgu, wd, wgu_s, wd_s = s["wgu"], s["wd"], s["wgu_s"], s["wd_s"]
     comb, mix = s["comb"], s["mix"]
 
@@ -193,8 +206,12 @@
     zl, core = h // 2, h % 2
     x, zh = expert // 2, expert % 2
     g = zh * 8 + h
-    def ring_id(gg):
-        return (y * 8 + gg % 8, x * 2 + gg // 8)
+    near, far = zl + 1 - 2 * (zl % 2), (zl + 2) % LINE
+    cross = (near + 2) % LINE
+    order = (cross, near, far, zl)
+
+    def ring_id(gg, section=y):
+        return (section * 8 + gg % 8, x * 2 + gg // 8)
 
     def x_id(xx):
         return (pipe, xx * 2 + zh)
@@ -206,7 +223,7 @@
         return (x + XN - i) % XN
 
     sib_id = (pipe + 1 - 2 * core, expert)
-    ends = (((pipe + 8) % 64, expert), ((pipe + 56) % 64, expert))
+    after = ((y + 1) % 8, (y + 7) % 8)
 
     def remote(src, dst, ss, rs, dev):
         return pltpu.make_async_remote_copy(
@@ -249,11 +266,23 @@
 
     def rs_copy(st, q, k):
         src, dst = piece("rs_s", st, q).at[k], piece("rs_r", st, q).at[k]
-        return remote(src, dst, *pair("rs" + st[1], st[0], q, k), line_id((zl + SHIFTS[k]) % LINE))
+        return remote(src, dst, *pair("rs" + st[1], st[0], q, k), line_id(order[k]))
+
+    def near_copy(st, q):
+        src, dst = piece("na_s", st, q), piece("na_r", st, q)
+        return remote(src, dst, *pair("na", st[0], q), line_id(near))
+
+    def far_copy(st, q):
+        src, dst = piece("fa_s", st, q), piece("fa_r", st, q)
+        return remote(src, dst, *pair("fa", st[0], q), line_id(far))
 
     def ag_copy(st, q, k):
         here = units_of(st, q).at[core, :, :, block_at(zl)]
-        return remote(here, here, *pair("ag" + st[1], st[0], q, k), line_id((zl + SHIFTS[k]) % LINE))
+        return remote(here, here, *pair("ag" + st[1], st[0], q, k), line_id(order[k]))
+
+    def relay_copy(st, q):
+        here = units_of(st, q).at[core, :, :, block_at(far)]
+        return remote(here, here, *pair("agn", st[0], q, 0), line_id(near))
 
     def as_copy(st, q):
         here = units_of(st, q).at[core]
@@ -275,10 +304,18 @@
     def w_copy(st, d):
         t, kind = st
         to = (g + d) % ZN
-        return remote(s["wsend" + kind].at[t, to], s["wrecv" + kind].at[t, g], *pair("w" + kind, t, d), ring_id(to))
-
-    def y_copy(t):
-        return remote(comb.at[t], (out_f, out_b)[t], *pair("y", t), ends[t])
+        src, dst = s["wsend" + kind].at[t, to], s["wrecv" + kind].at[t, g]
+        return remote(src, dst, *pair("w" + kind, t, d), ring_id(to, after[t]))
+
+    def choices(t):
+        dev = ring_id(g, after[t])
+        return [
+            remote((r_f, r_b)[t], s["rn_v"].at[t], *pair("y", t, 0), dev),
+            remote((g_f, g_b)[t], s["gn_v"].at[t], *pair("y", t, 1), dev),
+        ]
+
+    def out_copy(t):
+        return pltpu.make_async_copy(comb.at[t], (out_f, out_b)[t], s["out_sem"].at[t])
 
     wx = [
         remote(wgu_h.at[:, :, 1 - core], wgu_s, *pair("wx", 0), sib_id),
@@ -286,7 +323,7 @@
     ]
 
     moves = (
-        (r_b, r_v.at[B]), (x_b, xin.at[B]), (r_f, r_v.at[F]), (x_f, xin.at[F]), (g_f, g_v.at[F]), (g_b, g_v.at[B]),
+        (r_b, r_v.at[B]), (x_b, xin.at[B]), (r_f, r_v.at[F]), (x_f, xin.at[F]),
         (saved_h, s["saved"]), (wgu_h, wgu), (wd_h, wd),
     )
     loads = [pltpu.make_async_copy(a, b, s["load_sem"].at[i]) for i, (a, b) in enumerate(moves)]
@@ -296,11 +333,11 @@
     barrier = pltpu.get_barrier_semaphore()
     peers = [ring_id((g + d) % ZN) for d in range(1, ZN)]
     peers += [x_id((x + d) % XN) for d in range(1, XN)]
-    peers += list(ends)
+    peers += [ring_id(gg, section) for section in after for gg in range(ZN)]
     for peer in peers:
         pl.semaphore_signal(barrier, inc=1, device_id=peer, device_id_type=MESH)
 
-    for load in loads[:6]:
+    for load in loads[:4]:
         load.wait()
     routing = {}
     for t in (B, F):
@@ -310,7 +347,7 @@
         pick = jnp.where(match[0] | match[1], 1.0, 0.0).astype(jnp.bfloat16)
         name = lax.broadcasted_iota(jnp.int32, (8, 1), 0)
         mine = jnp.sum(jnp.where(name == expert, counts, 0.0), axis=0, keepdims=True)
-        routing[t] = (route, ranks, mine > BASE + 0.5)
+        routing[t] = mine > BASE + 0.5
         upper = lax.broadcasted_iota(jnp.int32, (16, 256), 0) < 8
         for b in range(8):
             rows = dot(pick, xin[t, :, b * 512 : (b + 1) * 512])
@@ -320,7 +357,7 @@
                 s["zsendo"][t, hi * 8 + b] = over
 
     def busiest_only(t, value):
-        return jnp.where(routing[t][2], value, 0.0)
+        return jnp.where(routing[t], value, 0.0)
 
     pl.semaphore_wait(barrier, len(peers))
 
@@ -334,13 +371,16 @@
     for copy in wx:
         copy.start()
     rows_to_ring(STREAMS[1])
+    for t in (B, F):
+        for copy in choices(t):
+            copy.start()
 
     s["c_no"][...] = norm_out()
     s["c_nb"][...] = norm_back()
     for half in range(2):
         s["c_oo"][half] = over_out(half)
         s["c_ob"][half] = over_back(half)
-    loads[6].wait()
+    loads[4].wait()
     for i in range(XN):
         found = dot(stash_rows(chunk_of(i)), s["saved"][...])
         s["kept_n"][i // 2, (i % 2) * NORM : (i % 2 + 1) * NORM] = found[:NORM]
@@ -375,19 +415,19 @@
     rows_to_ring(STREAMS[2])
     rows_to_ring(STREAMS[3])
 
-    for load in loads[7:]:
-        load.wait()
-    for copy in wx:
-        copy.wait_recv()
-    for k, shift in enumerate(SHIFTS):
-        dest = (zl + shift) % LINE
-        at = k * 128
-        s["up_b"][0, :, at : at + 128] = jnp.transpose(wd[dest, core])
-        s["up_b"][1, :, at : at + 128] = jnp.transpose(wd_s[dest])
-        for a in range(2):
-            at = k * 256 + a * 128
-            s["up_f"][0, :, at : at + 128] = jnp.transpose(wgu[a, dest, core])
-            s["up_f"][1, :, at : at + 128] = jnp.transpose(wgu_s[a, dest])
+    def turn_weights():
+        for load in loads[5:]:
+            load.wait()
+        for copy in wx:
+            copy.wait_recv()
+        for k, dest in enumerate(order):
+            at = k * 128
+            s["up_b"][0, :, at : at + 128] = jnp.transpose(wd[dest, core])
+            s["up_b"][1, :, at : at + 128] = jnp.transpose(wd_s[dest])
+            for a in range(2):
+                at = k * 256 + a * 128
+                s["up_f"][0, :, at : at + 128] = jnp.transpose(wgu[a, dest, core])
+                s["up_f"][1, :, at : at + 128] = jnp.transpose(wgu_s[a, dest])
 
     def products(st):
         t, kind = st
@@ -409,11 +449,12 @@
                 continue
             for q in range(2):
                 rows = part[q * 2 * NORM : (q + 1) * 2 * NORM]
-                if k == 3:
-                    piece("own", st, q)[...] = rows
+                if k < 2:
+                    piece("na_s", st, q)[k] = rows.astype(jnp.bfloat16)
+                    if k == 1:
+                        near_copy(st, q).start()
                 else:
-                    piece("rs_s", st, q)[k] = rows.astype(jnp.bfloat16)
-                    rs_copy(st, q, k).start()
+                    piece("own", st, q)[k - 2] = rows
         if kind == "o":
             for i in (2, 1, 3):
                 xr_copy(t, i).start()
@@ -427,17 +468,29 @@
             for i in range(1, XN):
                 total = total + s[f"xr_r{t}"][i, k].astype(jnp.float32)
             if k == 3:
-                piece("own", st, 0)[...] = total
+                piece("own", st, 0)[1] = total
             else:
                 piece("rs_s", st, 0)[k] = total.astype(jnp.bfloat16)
                 rs_copy(st, 0, k).start()
 
+    def pass_on(st):
+        for q in range(2):
+            near_copy(st, q).wait_recv()
+            total = piece("own", st, q)[0] + piece("na_r", st, q)[0].astype(jnp.float32)
+            piece("fa_s", st, q)[...] = total.astype(jnp.bfloat16)
+            far_copy(st, q).start()
+
     def activate(st):
         for q in range(PIECES[st[1]]):
-            total = piece("own", st, q)[...]
-            for k in range(3):
-                rs_copy(st, q, k).wait_recv()
-                total = total + piece("rs_r", st, q)[k].astype(jnp.float32)
+            total = piece("own", st, q)[1]
+            if st[1] == "n":
+                far_copy(st, q).wait_recv()
+                total = total + piece("na_r", st, q)[1].astype(jnp.float32)
+                total = total + piece("fa_r", st, q)[...].astype(jnp.float32)
+            else:
+                for k in range(3):
+                    rs_copy(st, q, k).wait_recv()
+                    total = total + piece("rs_r", st, q)[k].astype(jnp.float32)
             hid = units_of(st, q)
             if st[0] == F:
                 gate, up = total[:, :128], total[:, 128:]
@@ -449,13 +502,22 @@
                 slope = sig * (1.0 + gate * (1.0 - sig))
                 hid[core, 0, :, block_at(zl)] = (total * up * slope).astype(jnp.bfloat16)
                 hid[core, 1, :, block_at(zl)] = (total * (gate * sig)).astype(jnp.bfloat16)
-            for k in range(3):
+            for k in (2, 1) if st[1] == "n" else (2, 1, 0):
                 ag_copy(st, q, k).start()
+
+    def relay(st):
+        for q in range(2):
+            ag_copy(st, q, 2).wait_recv()
+            relay_copy(st, q).start()
 
     def units_to_sibling(st):
         for q in range(PIECES[st[1]]):
-            for k in range(3):
-                ag_copy(st, q, k).wait_recv()
+            ag_copy(st, q, 1).wait_recv()
+            if st[1] == "n":
+                relay_copy(st, q).wait_recv()
+            else:
+                ag_copy(st, q, 2).wait_recv()
+                ag_copy(st, q, 0).wait_recv()
             as_copy(st, q).start()
         if st[1] == "o":
             for i in (2, 1, 3):
@@ -517,20 +579,23 @@
         else:
             moved = dot(s["c_ob"][0], got[:, :256]) + dot(s["c_ob"][1], got[:, 256:])
         s["wsend" + kind][t] = moved.astype(jnp.bfloat16).reshape(ZN, 16, WIDTH[kind])
-        for d in range(1, ZN):
+        for d in W_ORDER:
             w_copy(st, d).start()
-        s["wrecv" + kind][t, g] = s["wsend" + kind][t, g]
 
     begun = set()
 
     def combine(st):
         t, kind = st
-        route, ranks, _ = routing[t]
-        for d in range(1, ZN):
+        if t not in begun:
+            for copy in choices(t):
+                copy.wait_recv()
+        route = s["rn_v"][t]
+        ranks, _ = route_ranks(route)
+        for d in W_ORDER:
             w_copy(st, d).wait_recv()
         got = s["wrecv" + kind]
         for half in range(2):
-            parts = gate_parts(route, g_v[t], ranks, half)
+            parts = gate_parts(route, s["gn_v"][t], ranks, half)
             parts = parts[:, 0:32] if kind == "n" else parts[:, 32:64]
             for b in range(8):
                 rows = jnp.concatenate([got[t, b], got[t, 8 + b]], axis=0)
@@ -544,7 +609,7 @@
                 else:
                     mix[t, :, at] = mixed
         if t in begun:
-            y_copy(t).start()
+            out_copy(t).start()
         begun.add(t)
 
     def late_stash(st):
@@ -557,19 +622,23 @@
     first = [rows_to_x, rows_to_sibling, products]
     last = [back_to_x, rows_to_sources, combine]
     steps = {
-        "n": first + [activate, units_to_sibling] + last,
+        "n": first + [pass_on, activate, relay, units_to_sibling] + last,
         "o": first + [late_stash, activate, units_to_sibling, spread_units] + last,
     }
-    for turn in range(len(steps["o"]) + max(LAG)):
-        for st, lag in zip(STREAMS, LAG):
-            if 0 <= turn - lag < len(steps[st[1]]):
-                steps[st[1]][turn - lag](st)
+    turned = False
+    for at in ORDER:
+        st = STREAMS[at // 10]
+        steps[st[1]][at % 10](st)
+        if at % 10 == 1 and not turned:
+            turn_weights()
+            turned = True
 
     for copy in wx:
         copy.wait_send()
     for st in STREAMS:
         for d in range(1, ZN):
             z_copy(st, d).wait_send()
+        for d in W_ORDER:
             w_copy(st, d).wait_send()
         for i in range(XN):
             c_copy(st, i).wait_send()
@@ -578,16 +647,25 @@
             b_copy(st, i).wait_send()
         for q in range(PIECES[st[1]]):
             as_copy(st, q).wait_send()
-            for k in range(3):
-                rs_copy(st, q, k).wait_send()
-                ag_copy(st, q, k).wait_send()
+            ag_copy(st, q, 1).wait_send()
+            ag_copy(st, q, 2).wait_send()
+            if st[1] == "n":
+                near_copy(st, q).wait_send()
+                far_copy(st, q).wait_send()
+                relay_copy(st, q).wait_send()
+            else:
+                ag_copy(st, q, 0).wait_send()
+                for k in range(3):
+                    rs_copy(st, q, k).wait_send()
     for i in range(1, XN):
         sv_copy(i).wait_send()
         for t in (B, F):
             for copy in (xr_copy, xg_copy, xa_copy):
                 copy(t, i).wait_send()
     for t in (B, F):
-        y_copy(t).wait()
+        for copy in choices(t):
+            copy.wait_send()
+        out_copy(t).wait()
 
 
 def on_device(x_f, r_f, g_f, x_b, r_b, g_b, gate_up, down, saved):

time: 123 us -> 113 us (0.919)
  Pallas kernels: 119 us -> 109 us
    pallas_call x1, Pallas kernels: 119 us -> 109 us  [on_device(): call(x_f[0], r_f[0].T, g_f[0].T, x_b[0], r_b[0].T, g_b[0].T, gate_up.resh...]
where the time goes in v4:
time: 113 us
  Pallas kernels  109 us (96%)
  local copies, waits for them, and re-layouts  3.14 us (3%)
    pallas_call x1, Pallas kernels, on_device(): call(x_f[0], r_f[0].T, g_f[0].T, x_b[0], r_b[0].T, g_b[0].T, gate_up.resh...  109 us
    unnamed x2, local copies, waits for them, and re-layouts  3.14 us

profile of v4, /device:TPU:1, one launch (start us, length us, event | category | flops | bytes accessed | tf_op | source)
XLA Modules:
  0.0 112.6 jit_solution(13266823786590067587)
XLA Ops:
  0.6 108.8 %shard_map.104 = (bf16[16,4096]{1,0:T(8,128)(2,1)}, bf16[16,4096]{1,0:T(8,128)(2,1)}) custom-call(bf16[16,4096]{1,0:T(8,128)(2,1)} %bitcast.24, s32[2,16]{1,0:T(2,128)} %bitcast.26, f32[2,16]{1,0:T(2,128)} %bitcast.27, bf16[16,4096]{1,0:T(8,128)(2,1)} %bitcast.25, s32[2,16]{1,0:T(2,128)} %bitcast.28, f32[2,16]{1,0:T(2,128)} %bitcast.29, ...), custom_call_target="tpu_custom_call" | custom-call | flops 4000000000 | bytes 8000000 | tf_op jit(solution)/shard_map/pallas_call | solution.py:685
  109.5 1.6 %copy.13 = bf16[1,16,4096]{2,1,0:T(8,128)(2,1)} copy(bf16[1,16,4096]{2,1,0:T(8,128)(2,1)} %bitcast.20) | data formatting | bytes 262144
  111.0 1.6 %copy.14 = bf16[1,16,4096]{2,1,0:T(8,128)(2,1)} copy(bf16[1,16,4096]{2,1,0:T(8,128)(2,1)} %bitcast.19) | data formatting | bytes 262144

commit v5 on v4

--- a/solution.py
+++ b/solution.py
@@ -20,11 +20,12 @@
 STREAMS = ((B, "o"), (B, "n"), (F, "o"), (F, "n"))
 Z_ORDER = (8, 7, 9, 6, 10, 5, 11, 4, 12, 3, 13, 2, 14, 1, 15)
 W_ORDER = Z_ORDER + (0,)
+ENTRY = (3, 0, 1, 2)
 ORDER = (
-    0, 10, 1, 2, 11, 30, 12, 20, 3, 31,
-    13, 32, 4, 21, 22, 14, 33, 23, 5, 15,
-    34, 24, 16, 35, 17, 25, 36, 6, 37, 18,
-    7, 26, 27, 38, 8, 28, 39, 19, 9, 29,
+    30, 0, 31, 10, 32, 20, 1, 2, 11, 33,
+    21, 12, 22, 3, 34, 13, 4, 35, 23, 36,
+    14, 5, 24, 37, 15, 6, 25, 7, 16, 38,
+    17, 26, 27, 8, 18, 28, 19, 39, 9, 29,
 )
 PIECES = {"n": 2, "o": 1}
 MESH = pl.DeviceIdType.MESH
@@ -331,7 +332,7 @@
         load.start()
 
     barrier = pltpu.get_barrier_semaphore()
-    peers = [ring_id((g + d) % ZN) for d in range(1, ZN)]
+    peers = [ring_id((g + d) % ZN) for d in Z_ORDER]
     peers += [x_id((x + d) % XN) for d in range(1, XN)]
     peers += [ring_id(gg, section) for section in after for gg in range(ZN)]
     for peer in peers:
@@ -367,10 +368,10 @@
             z_copy(st, d).start()
         s["zrecv" + kind][t, g] = s["zsend" + kind][t, g]
 
-    rows_to_ring(STREAMS[0])
+    rows_to_ring(STREAMS[ENTRY[0]])
     for copy in wx:
         copy.start()
-    rows_to_ring(STREAMS[1])
+    rows_to_ring(STREAMS[ENTRY[1]])
     for t in (B, F):
         for copy in choices(t):
             copy.start()
@@ -412,8 +413,8 @@
             x_copy(st, i).wait_recv()
             c_copy(st, i).start()
 
-    rows_to_ring(STREAMS[2])
-    rows_to_ring(STREAMS[3])
+    rows_to_ring(STREAMS[ENTRY[2]])
+    rows_to_ring(STREAMS[ENTRY[3]])
 
     def turn_weights():
         for load in loads[5:]:
@@ -629,7 +630,7 @@
     for at in ORDER:
         st = STREAMS[at // 10]
         steps[st[1]][at % 10](st)
-        if at % 10 == 1 and not turned:
+        if at % 10 == 0 and not turned:
             turn_weights()
             turned = True
 

time: 113 us -> 110 us (0.973)
  the two profiles are of different devices: /device:TPU:1 before, /device:TPU:17 now
where the time goes in v5:
time: 110 us
  Pallas kernels  106 us (96%)
  local copies, waits for them, and re-layouts  3.14 us (3%)
    pallas_call x1, Pallas kernels, on_device(): call(x_f[0], r_f[0].T, g_f[0].T, x_b[0], r_b[0].T, g_b[0].T, gate_up.resh...  106 us
    unnamed x2, local copies, waits for them, and re-layouts  3.14 us

profile of v5, /device:TPU:17, one launch (start us, length us, event | category | flops | bytes accessed | tf_op | source)
XLA Modules:
  0.0 110.0 jit_solution(10720958611881833797)
XLA Ops:
  0.6 106.2 %shard_map.104 = (bf16[16,4096]{1,0:T(8,128)(2,1)}, bf16[16,4096]{1,0:T(8,128)(2,1)}) custom-call(bf16[16,4096]{1,0:T(8,128)(2,1)} %bitcast.24, s32[2,16]{1,0:T(2,128)} %bitcast.26, f32[2,16]{1,0:T(2,128)} %bitcast.27, bf16[16,4096]{1,0:T(8,128)(2,1)} %bitcast.25, s32[2,16]{1,0:T(2,128)} %bitcast.28, f32[2,16]{1,0:T(2,128)} %bitcast.29, ...), custom_call_target="tpu_custom_call" | custom-call | flops 4000000000 | bytes 8000000 | tf_op jit(solution)/shard_map/pallas_call | solution.py:686
  106.8 1.6 %copy.13 = bf16[1,16,4096]{2,1,0:T(8,128)(2,1)} copy(bf16[1,16,4096]{2,1,0:T(8,128)(2,1)} %bitcast.20) | data formatting | bytes 262144
  108.4 1.6 %copy.14 = bf16[1,16,4096]{2,1,0:T(8,128)(2,1)} copy(bf16[1,16,4096]{2,1,0:T(8,128)(2,1)} %bitcast.19) | data formatting | bytes 262144

commit v6 on v5

--- a/solution.py
+++ b/solution.py
@@ -195,7 +195,7 @@
     return out
 
 
-def kernel(x_f, r_f, g_f, x_b, r_b, g_b, wgu_h, wd_h, saved_h, out_f, out_b, *scratch):
+def kernel(x_f, r_f, g_f, x_b, r_b, g_b, wgu_h, wd_h, saved_h, out, *scratch):
     s = dict(zip(buffers(), scratch))
     xin, r_v = s["xin"], s["r_v"]
     wgu, wd, wgu_s, wd_s = s["wgu"], s["wd"], s["wgu_s"], s["wd_s"]
@@ -316,7 +316,7 @@
         ]
 
     def out_copy(t):
-        return pltpu.make_async_copy(comb.at[t], (out_f, out_b)[t], s["out_sem"].at[t])
+        return pltpu.make_async_copy(comb.at[t], out.at[t], s["out_sem"].at[t])
 
     wx = [
         remote(wgu_h.at[:, :, 1 - core], wgu_s, *pair("wx", 0), sib_id),
@@ -671,23 +671,22 @@
 
 def on_device(x_f, r_f, g_f, x_b, r_b, g_b, gate_up, down, saved):
     in_hbm = pl.BlockSpec(memory_space=pltpu.HBM)
-    out = jax.ShapeDtypeStruct((16, 4096), jnp.bfloat16)
     call = pl.pallas_call(
         kernel,
-        out_shape=[out, out],
+        out_shape=jax.ShapeDtypeStruct((2, 16, 4096), jnp.bfloat16),
         in_specs=[in_hbm] * 9,
-        out_specs=[in_hbm, in_hbm],
+        out_specs=in_hbm,
         scratch_shapes=list(buffers().values()),
         compiler_params=pltpu.CompilerParams(
             collective_id=0, has_side_effects=True, vmem_limit_bytes=60 * 1024 * 1024
         ),
         cost_estimate=pl.CostEstimate(flops=4 * 10**9, bytes_accessed=8 * 10**6, transcendentals=10**6),
     )
-    next_input, prior_gradient = call(
+    both = call(
         x_f[0], r_f[0].T, g_f[0].T, x_b[0], r_b[0].T, g_b[0].T,
         gate_up.reshape(2, 4, 2, 128, 512), down.reshape(4, 2, 128, 512), saved[0, 0],
     )
-    return next_input[None], prior_gradient[None]
+    return both[F : F + 1], both[B : B + 1]
 
 
 def solution(mesh):

time: 110 us -> 109 us (level)
  local copies, waits for them, and re-layouts: 3.14 us -> 1.68 us
    unnamed x2 -> x0, local copies, waits for them, and re-layouts: 3.14 us -> none
    slice x0 -> x1, local copies, waits for them, and re-layouts: none -> 1.68 us  [on_device(): return (both[F:F + 1], both[B:B + 1])]
where the time goes in v6:
time: 109 us
  Pallas kernels  106 us (97%)
  local copies, waits for them, and re-layouts  1.68 us (2%)
    pallas_call x1, Pallas kernels, on_device(): call(x_f[0], r_f[0].T, g_f[0].T, x_b[0], r_b[0].T, g_b[0].T, gate_up.resh...  106 us

profile of v6, /device:TPU:17, one launch (start us, length us, event | category | flops | bytes accessed | tf_op | source)
XLA Modules:
  0.0 108.6 jit_solution(16971184811876381728)
XLA Ops:
  0.6 106.3 %shard_map.104 = bf16[2,16,4096]{2,1,0:T(8,128)(2,1)} custom-call(bf16[16,4096]{1,0:T(8,128)(2,1)} %bitcast.20, s32[2,16]{1,0:T(2,128)} %bitcast.22, f32[2,16]{1,0:T(2,128)} %bitcast.23, bf16[16,4096]{1,0:T(8,128)(2,1)} %bitcast.21, s32[2,16]{1,0:T(2,128)} %bitcast.24, f32[2,16]{1,0:T(2,128)} %bitcast.25, bf16[2,4,2,128,512]{4,3,2,1,0:T(8,128)(2,1)} %bitcast.17, ...), custom_call_target="tpu_custom_call" | custom-call | flops 4000000000 | bytes 8000000 | tf_op jit(solution)/shard_map/pallas_call | solution.py:685
  106.9 1.7 %fusion = (bf16[1,16,4096]{2,1,0:T(8,128)(2,1)}, bf16[1,16,4096]{2,1,0:T(8,128)(2,1)}) fusion(bf16[2,16,4096]{2,1,0:T(8,128)(2,1)} %shard_map.104), kind=kLoop, calls=%fused_computation | loop fusion | bytes 524288 | tf_op jit(solution)/shard_map/slice | solution.py:689
